TPU v7x, 768 devices: a whole 4x8x12 slice. The times are simulated.
768 devices in a mesh: dp: 16 (over z_lo, x), rows: 48 (over z_hi, y, core).
Axes of the slice: x: 4, y: 8, z: 12 (z_hi: 3, z_lo: 4; z = z_hi * 4 + z_lo), core: 2. Of those that a mesh axis runs over, the one named last changes fastest.
Arguments:
- images: float32 [196608, 1152], P(('dp', 'rows')), may hold values from -0.2 to 0.2
- texts: float32 [196608, 1152], P(('dp', 'rows')), may hold values from -0.2 to 0.2
- log_temp: float32 [1], replicated, may hold values from 0.7 to 1.8
- bias: float32 [1], replicated, may hold values from -3 to -1
Outputs:
- row_loss: float32 [196608], P(('dp', 'rows'))
- image_grad: float32 [196608, 1152], P(('dp', 'rows'))
- text_grad: float32 [196608, 1152], P(('dp', 'rows'))
All inputs are finite; a program needn't handle non-finite values.
Results may differ from a plain program's by a relative error of at most 0.0091.
Values may be sent and summed in bfloat16 or wider, within the bound.
No kernel may reach another device: no remote copies, remote signals or barrier semaphores. Data moves between devices by JAX's collectives and lax.ppermute only.
A program may use at most 32 MiB of HBM per device.

v0:
```python
import jax
import jax.numpy as jnp
from jax import lax
from jax.sharding import PartitionSpec as P

STEPS = 4


def from_behind(value, axis, steps):
    count = lax.axis_size(axis)
    pairs = [(source, (source + steps) % count) for source in range(count)]
    return lax.ppermute(value, axis, pairs)


def unit_rows(values):
    norms = jnp.sqrt(jnp.sum(values * values, axis=-1, keepdims=True) + 1e-06)
    return (values / norms, norms)


def back_rows(unit, norms, grad_unit):
    along = jnp.sum(unit * grad_unit, axis=-1, keepdims=True)
    return (grad_unit - unit * along) / norms


def local(images, texts, log_temp, bias):
    scale = jnp.exp(log_temp[0])
    shift_b = bias[0]
    img_unit, img_norm = unit_rows(images)
    txt_unit, txt_norm = unit_rows(texts)
    img_half = img_unit.astype(jnp.bfloat16)
    txt_half = txt_unit.astype(jnp.bfloat16)
    count = images.shape[0]
    eye = jnp.eye(count, dtype=jnp.float32)

    def tile_grad(left, visit, first):
        logits = scale * jnp.dot(left, visit.T, preferred_element_type=jnp.float32) + shift_b
        sign = 2.0 * eye - 1.0 if first else -jnp.ones_like(eye)
        loss_part = jnp.sum(jax.nn.softplus(-sign * logits), axis=-1)
        dlogit = (-sign * jax.nn.sigmoid(-sign * logits) * scale).astype(jnp.bfloat16)
        return (loss_part, dlogit)

    def score_tile(visit, first):
        loss_part, dlogit = tile_grad(img_half, visit, first)
        img_part = jnp.dot(dlogit, visit, preferred_element_type=jnp.float32)
        txt_part = jnp.dot(dlogit.T, img_half, preferred_element_type=jnp.float32)
        return (loss_part, img_part, txt_part)

    loss_sum, img_grad_unit, own_txt = score_tile(txt_half, True)
    current = txt_half
    carried = own_txt
    for step in range(1, STEPS):
        current = from_behind(current, ("dp", "rows"), 1)
        carried = from_behind(carried, ("dp", "rows"), 1)
        loss_part, img_part, txt_part = score_tile(current, False)
        loss_sum = loss_sum + loss_part
        img_grad_unit = img_grad_unit + img_part
        carried = carried + txt_part
    txt_grad_unit = from_behind(carried, ("dp", "rows"), 1 - STEPS)
    row_loss = loss_sum / (STEPS * count)
    image_grad = back_rows(img_unit, img_norm, img_grad_unit)
    text_grad = back_rows(txt_unit, txt_norm, txt_grad_unit)
    return (row_loss, image_grad, text_grad)


def solution(mesh):
    placed = (P(("dp", "rows"), None), P(("dp", "rows"), None), P(), P())
    return jax.shard_map(
        local,
        mesh=mesh,
        in_specs=placed,
        out_specs=(P(("dp", "rows")), P(("dp", "rows"), None), P(("dp", "rows"), None)),
        check_vma=False,
    )
```

profile of v0, /device:TPU:64, one launch (start us, length us, event | category | flops | bytes accessed | tf_op | source)
XLA Modules:
  0.0 319.1 jit_solution(6576770785602602936)
XLA Ops:
  0.6 0.0 copy-start.1
  1.4 1.4 multiply_reduce_fusion.3
  2.8 0.0 copy-start
  2.8 0.0 copy-done.1
  2.8 0.1 fusion.13
  3.0 1.1 copy-done
  4.1 0.2 multiply_reduce_fusion.2
  4.3 0.2 fusion.14
  5.1 0.5 fusion.5
  5.6 0.4 fusion.11
  6.0 1.9 collective-permute-start.3
  7.9 3.6 %collective-permute-start = (bf16[256,1152]{1,0:T(8,128)(2,1)S(1)}, bf16[256,1152]{1,0:T(8,128)(2,1)S(1)}, u32[]{:S(2)}, u32[]{:S(2)}) collective-permute-start(bf16[256,1152]{1,0:T(8,128)(2,1)S(1)} %fusion.14), channel_id=1, source_target_pairs={{0,1},{1,2},{2,3},{3,4},{4,5},{5,6},{6,7},{7,8},{8,9},{9,10},{10,1... | collective-permute-start | bytes 1769480 | tf_op jit(solution)/shard_map/ppermute | solution.py:12
  11.5 77.3 %collective-permute-done = bf16[256,1152]{1,0:T(8,128)(2,1)S(1)} collective-permute-done((bf16[256,1152]{1,0:T(8,128)(2,1)S(1)}, bf16[256,1152]{1,0:T(8,128)(2,1)S(1)}, u32[]{:S(2)}, u32[]{:S(2)}) %collective-permute-start) | collective-permute-done | bytes 589856 | tf_op jit(solution)/shard_map/ppermute | solution.py:12
  88.8 0.5 fusion.6
  89.3 0.0 collective-permute-done.3
  89.3 0.4 convolution_add_fusion
  89.7 1.9 collective-permute-start.4
  91.6 1.9 collective-permute-start.1
  93.5 87.1 %collective-permute-done.1 = bf16[256,1152]{1,0:T(8,128)(2,1)S(1)} collective-permute-done((bf16[256,1152]{1,0:T(8,128)(2,1)S(1)}, bf16[256,1152]{1,0:T(8,128)(2,1)S(1)}, u32[]{:S(2)}, u32[]{:S(2)}) %collective-permute-start.1) | collective-permute-done | bytes 589856 | tf_op jit(solution)/shard_map/ppermute | solution.py:12
  180.6 0.5 fusion.7
  181.1 0.4 fusion.9
  181.5 0.0 collective-permute-done.4
  181.5 0.1 add.109
  181.6 1.9 collective-permute-start.5
  183.5 0.4 fusion.12
  184.0 1.9 collective-permute-start.2
  185.9 0.4 convolution_add_fusion.3
  186.3 0.4 convolution_add_fusion.2
  186.7 74.1 %collective-permute-done.2 = bf16[256,1152]{1,0:T(8,128)(2,1)S(1)} collective-permute-done((bf16[256,1152]{1,0:T(8,128)(2,1)S(1)}, bf16[256,1152]{1,0:T(8,128)(2,1)S(1)}, u32[]{:S(2)}, u32[]{:S(2)}) %collective-permute-start.2) | collective-permute-done | bytes 589856 | tf_op jit(solution)/shard_map/ppermute | solution.py:12
  260.8 0.5 fusion.8
  261.3 0.4 fusion.10
  261.6 0.0 collective-permute-done.5
  261.7 0.1 add.110
  261.8 1.9 collective-permute-start.6
  263.7 0.6 add_multiply_fusion
  264.3 0.5 multiply_reduce_fusion.1
  264.8 1.3 subtract_divide_fusion.1
  266.1 51.6 %collective-permute-done.6 = f32[256,1152]{1,0:T(8,128)S(1)} collective-permute-done((f32[256,1152]{1,0:T(8,128)S(1)}, f32[256,1152]{1,0:T(8,128)S(1)}, u32[]{:S(2)}, u32[]{:S(2)}) %collective-permute-start.6) | collective-permute-done | bytes 1179680 | tf_op jit(solution)/shard_map/ppermute | solution.py:12
  317.6 0.3 multiply_reduce_fusion
  317.9 1.3 subtract_divide_fusion
  (2 shorter events, 0.0 us)
Async XLA Ops:
  0.6 2.2 copy-start.1
  2.8 1.3 copy-start
  6.0 83.3 %collective-permute-start.3 = (f32[256,1152]{1,0:T(8,128)S(1)}, f32[256,1152]{1,0:T(8,128)S(1)}, u32[]{:S(2)}, u32[]{:S(2)}) collective-permute-start(f32[256,1152]{1,0:T(8,128)S(1)} %fusion.11), channel_id=1, source_target_pairs={{0,1},{1,2},{2,3},{3,4},{4,5},{5,6},{6,7},{7,8},{8,9},{9,10},{10,1... | collective-permute-start | bytes 3538952 | tf_op jit(solution)/shard_map/ppermute | solution.py:12
  7.9 80.9 %collective-permute-start = (bf16[256,1152]{1,0:T(8,128)(2,1)S(1)}, bf16[256,1152]{1,0:T(8,128)(2,1)S(1)}, u32[]{:S(2)}, u32[]{:S(2)}) collective-permute-start(bf16[256,1152]{1,0:T(8,128)(2,1)S(1)} %fusion.14), channel_id=1, source_target_pairs={{0,1},{1,2},{2,3},{3,4},{4,5},{5,6},{6,7},{7,8},{8,9},{9,10},{10,1... | collective-permute-start | bytes 1769480 | tf_op jit(solution)/shard_map/ppermute | solution.py:12
  89.7 91.8 %collective-permute-start.4 = (f32[256,1152]{1,0:T(8,128)S(1)}, f32[256,1152]{1,0:T(8,128)S(1)}, u32[]{:S(2)}, u32[]{:S(2)}) collective-permute-start(f32[256,1152]{1,0:T(8,128)S(1)} %convolution_add_fusion), channel_id=1, source_target_pairs={{0,1},{1,2},{2,3},{3,4},{4,5},{5,6},{6,7},{7,8},{8,9},{9,10},{10,1... | collective-permute-start | bytes 3538952 | tf_op jit(solution)/shard_map/ppermute | solution.py:12
  91.6 89.0 %collective-permute-start.1 = (bf16[256,1152]{1,0:T(8,128)(2,1)S(1)}, bf16[256,1152]{1,0:T(8,128)(2,1)S(1)}, u32[]{:S(2)}, u32[]{:S(2)}) collective-permute-start(bf16[256,1152]{1,0:T(8,128)(2,1)S(1)} %collective-permute-done), channel_id=1, source_target_pairs={{0,1},{1,2},{2,3},{3,4},{4,5},{5,6},{6,7},{7,8},{8,9},{9,10},{10,1... | collective-permute-start | bytes 1769480 | tf_op jit(solution)/shard_map/ppermute | solution.py:12
  181.6 80.0 %collective-permute-start.5 = (f32[256,1152]{1,0:T(8,128)S(1)}, f32[256,1152]{1,0:T(8,128)S(1)}, u32[]{:S(2)}, u32[]{:S(2)}) collective-permute-start(f32[256,1152]{1,0:T(8,128)S(1)} %add.109), channel_id=1, source_target_pairs={{0,1},{1,2},{2,3},{3,4},{4,5},{5,6},{6,7},{7,8},{8,9},{9,10},{10,1... | collective-permute-start | bytes 3538952 | tf_op jit(solution)/shard_map/ppermute | solution.py:12
  184.0 76.8 %collective-permute-start.2 = (bf16[256,1152]{1,0:T(8,128)(2,1)S(1)}, bf16[256,1152]{1,0:T(8,128)(2,1)S(1)}, u32[]{:S(2)}, u32[]{:S(2)}) collective-permute-start(bf16[256,1152]{1,0:T(8,128)(2,1)S(1)} %collective-permute-done.1), channel_id=1, source_target_pairs={{0,1},{1,2},{2,3},{3,4},{4,5},{5,6},{6,7},{7,8},{8,9},{9,10},{10,1... | collective-permute-start | bytes 1769480 | tf_op jit(solution)/shard_map/ppermute | solution.py:12
  261.8 55.8 %collective-permute-start.6 = (f32[256,1152]{1,0:T(8,128)S(1)}, f32[256,1152]{1,0:T(8,128)S(1)}, u32[]{:S(2)}, u32[]{:S(2)}) collective-permute-start(f32[256,1152]{1,0:T(8,128)S(1)} %add.110), channel_id=1, source_target_pairs={{0,765},{1,766},{2,767},{3,0},{4,1},{5,2},{6,3},{7,4},{8,5},{9,6},... | collective-permute-start | bytes 3538952 | tf_op jit(solution)/shard_map/ppermute | solution.py:12
where the time goes:
time: 320 us; the launch traced here: 319 us
  waiting for transfers between devices  290 us (91%)
  starting transfers between devices  15.1 us (5%)
  other arithmetic  5.51 us (2%)
  matrix products  5.22 us (2%)
    ppermute x7, waiting for transfers between devices, from_behind(): return lax.ppermute(value, axis, pairs)  290 us
    ppermute x7, starting transfers between devices, from_behind(): return lax.ppermute(value, axis, pairs)  15.1 us
  transfers between devices with their start and end apart: 7, of which 4 were waited for; matrix products, arithmetic and copies ran while one was open for 2% of the time, Pallas kernels for 0%

commit v1 on v0

v1 whole, which is shorter than its diff:
```python
import jax
import jax.numpy as jnp
from jax import lax
from jax.sharding import PartitionSpec as P

BAND = 4
AXES = ("dp", "rows")
X, Y, Z, CORES = 4, 8, 12, 2
COUNT = X * Y * Z * CORES
Z_LO, Z_HI = 4, 3


def place(k):
    core = k % CORES
    y = (k // CORES) % Y
    z_hi = (k // (CORES * Y)) % Z_HI
    x = (k // (CORES * Y * Z_HI)) % X
    z_lo = k // (CORES * Y * Z_HI * X)
    return x, y, z_hi * Z_LO + z_lo, core


INDEX = {place(k): k for k in range(COUNT)}


def routes():
    up, down, far, turn_near, turn_far, swap = [], [], [], [], [], []
    for k in range(COUNT):
        x, y, z, core = place(k)
        swap.append((k, k ^ 1))
        if core == 1 and y == Y - 1:
            stop = INDEX[(x, 0, z, 1)]
            up.append((k, stop))
            turn_near.append((stop, (k + 2) % COUNT))
            stop = INDEX[(x, 1, z, 0)]
            far.append((k, stop))
            turn_far.append((stop, (k + 3) % COUNT))
        else:
            up.append((k, (k + 2) % COUNT))
            if core == 1:
                far.append((k, (k + 3) % COUNT))
        if core == 0 and y == 0:
            stop = INDEX[(x, Y - 1, z, 0)]
            down.append((k, stop))
            turn_near.append((stop, (k - 2) % COUNT))
            stop = INDEX[(x, Y - 2, z, 1)]
            far.append((k, stop))
            turn_far.append((stop, (k - 3) % COUNT))
        else:
            down.append((k, (k - 2) % COUNT))
            if core == 0:
                far.append((k, (k - 3) % COUNT))
    return up, down, far, turn_near, turn_far, swap


def unit_rows(values):
    norms = jnp.sqrt(jnp.sum(values * values, axis=-1, keepdims=True) + 1e-06)
    return (values / norms, norms)


def back_rows(unit, norms, grad_unit):
    along = jnp.sum(unit * grad_unit, axis=-1, keepdims=True)
    return (grad_unit - unit * along) / norms


def send(value, pairs):
    return lax.ppermute(value, AXES, pairs)


def local(images, texts, log_temp, bias):
    up, down, far, turn_near, turn_far, swap = routes()
    scale = jnp.exp(log_temp[0])
    shift_b = bias[0]
    count = images.shape[0]
    place_rows = lax.axis_index("rows")
    core = place_rows % CORES
    y = (place_rows // CORES) % Y
    first = core == 0
    img_unit, img_norm = unit_rows(images)
    txt_unit, txt_norm = unit_rows(texts)
    img = img_unit.astype(jnp.bfloat16)
    txt = txt_unit.astype(jnp.bfloat16)

    txt_up = send(txt, up)
    img_down = send(img, down)
    far_in = send(jnp.where(first, img, txt), far)
    beside = send(jnp.where(first, txt, img), swap)
    turned = send(jnp.where(first, img_down, txt_up), turn_near)
    turned_far = send(far_in, turn_far)
    txt_2 = jnp.where((y == 0) & (core == 1), turned, txt_up)
    img_2 = jnp.where((y == Y - 1) & (core == 0), turned, img_down)
    far_3 = jnp.where(((y == 1) & (core == 0)) | ((y == Y - 2) & (core == 1)), turned_far, far_in)
    txt_other = send(txt_2, swap)
    img_other = send(img_2, swap)
    txt_last = jnp.where(first, far_3, beside)
    img_last = jnp.where(first, beside, far_3)

    eye = jnp.eye(count, dtype=jnp.float32)

    def tile(left, right, sign):
        logits = scale * jnp.dot(left, right.T, preferred_element_type=jnp.float32) + shift_b
        loss = jnp.sum(jax.nn.softplus(-sign * logits), axis=-1)
        dlogit = (-sign * jax.nn.sigmoid(-sign * logits) * scale).astype(jnp.bfloat16)
        return loss, dlogit

    loss_sum, dlogit = tile(img, txt, 2.0 * eye - 1.0)
    img_grad = jnp.dot(dlogit, txt, preferred_element_type=jnp.float32)
    txt_grad = jnp.dot(dlogit.T, img, preferred_element_type=jnp.float32)
    for visit in (txt_last, txt_2, txt_other):
        loss, dlogit = tile(img, visit, -1.0)
        loss_sum = loss_sum + loss
        img_grad = img_grad + jnp.dot(dlogit, visit, preferred_element_type=jnp.float32)
    for visit in (img_last, img_2, img_other):
        _, dlogit = tile(visit, txt, -1.0)
        txt_grad = txt_grad + jnp.dot(dlogit.T, visit, preferred_element_type=jnp.float32)
    row_loss = loss_sum / (BAND * count)
    image_grad = back_rows(img_unit, img_norm, img_grad)
    text_grad = back_rows(txt_unit, txt_norm, txt_grad)
    return (row_loss, image_grad, text_grad)


def solution(mesh):
    placed = (P(AXES, None), P(AXES, None), P(), P())
    return jax.shard_map(
        local,
        mesh=mesh,
        in_specs=placed,
        out_specs=(P(AXES), P(AXES, None), P(AXES, None)),
        check_vma=False,
    )
```

time: 320 us -> 117 us (0.37)
  the two profiles are of different devices: /device:TPU:64 before, /device:TPU:1 now
where the time goes in v1:
time: 117 us; the launch traced here: 116 us
  waiting for transfers between devices  45.1 us (39%)
  starting transfers between devices  33.8 us (29%)
  matrix products  24.7 us (21%)
  other arithmetic  10.4 us (9%)
  between operations  2.19 us (2%)
    ppermute x8, waiting for transfers between devices, send(): return lax.ppermute(value, AXES, pairs)  45.1 us
    ppermute x8, starting transfers between devices, send(): return lax.ppermute(value, AXES, pairs)  33.8 us
    dot_general x3, matrix products, local(): jnp.dot(dlogit.T, visit, preferred_element_type=jnp.float32)  9.42 us
    dot_general x4, matrix products, tile(): jnp.dot(left, right.T, preferred_element_type=jnp.float32)  6.74 us
    dot_general x3, matrix products, local(): jnp.dot(dlogit, visit, preferred_element_type=jnp.float32)  5.74 us
    div x2, other arithmetic, back_rows(): return (grad_unit - unit * along) / norms  2.54 us
  transfers between devices with their start and end apart: 8, of which 2 were waited for; matrix products, arithmetic and copies ran while one was open for 21% of the time, Pallas kernels for 0%

profile of v1, /device:TPU:1, one launch (start us, length us, event | category | flops | bytes accessed | tf_op | source)
XLA Modules:
  0.0 116.5 jit_solution(448227629835834407)
XLA Ops:
  0.6 0.0 copy-start
  0.7 0.0 copy-start.1
  0.7 1.6 %multiply_reduce_fusion.2 = f32[256]{0:T(256)S(1)} fusion(f32[256,1152]{1,0:T(8,128)} %param.5), kind=kLoop, calls=%fused_computation.10 | loop fusion | flops 589568 | bytes 1180672 | tf_op jit(solution)/shard_map/reduce_sum | solution.py:56
  2.3 0.0 copy-done
  2.3 0.2 multiply_reduce_fusion.3
  2.4 0.2 copy-done.1
  2.6 1.1 broadcast_select_fusion.5
  3.8 20.2 %collective-permute-start.3 = (bf16[256,1152]{1,0:T(8,128)(2,1)S(1)}, bf16[256,1152]{1,0:T(8,128)(2,1)S(1)}, u32[]{:S(2)}, u32[]{:S(2)}) collective-permute-start(bf16[256,1152]{1,0:T(8,128)(2,1)S(1)} %get-tuple-element.5), channel_id=1, source_target_pairs={{0,14},{1,767},{2,0},{3,1},{4,2},{5,3},{6,4},{7,5},{8,6},{9,7},{10... | collective-permute-start | bytes 1769480 | tf_op jit(solution)/shard_map/ppermute | solution.py:66
  24.0 1.9 %collective-permute-start.4 = (bf16[256,1152]{1,0:T(8,128)(2,1)S(1)}, bf16[256,1152]{1,0:T(8,128)(2,1)S(1)}, u32[]{:S(2)}, u32[]{:S(2)}) collective-permute-start(bf16[256,1152]{1,0:T(8,128)(2,1)S(1)} %get-tuple-element.4), channel_id=1, source_target_pairs={{0,2},{1,3},{2,4},{3,5},{4,6},{5,7},{6,8},{7,9},{8,10},{9,11},{10,... | collective-permute-start | bytes 1769480 | tf_op jit(solution)/shard_map/ppermute | solution.py:66
  25.9 0.1 broadcast_select_fusion.6
  26.0 1.9 %collective-permute-start = (bf16[256,1152]{1,0:T(8,128)(2,1)S(1)}, bf16[256,1152]{1,0:T(8,128)(2,1)}, u32[]{:S(2)}, u32[]{:S(2)}) collective-permute-start(bf16[256,1152]{1,0:T(8,128)(2,1)S(1)} %broadcast_select_fusion.6), channel_id=1, source_target_pairs={{0,13},{1,4},{2,767},{3,6},{4,1},{5,8},{6,3},{7,10},{8,5},{9,12},{... | collective-permute-start | bytes 1769480 | tf_op jit(solution)/shard_map/ppermute | solution.py:66
  27.9 1.9 %collective-permute-start.2 = (bf16[256,1152]{1,0:T(8,128)(2,1)}, bf16[256,1152]{1,0:T(8,128)(2,1)}, u32[]{:S(2)}, u32[]{:S(2)}) collective-permute-start(bf16[256,1152]{1,0:T(8,128)(2,1)} %get-tuple-element.3), channel_id=1, source_target_pairs={{0,1},{1,0},{2,3},{3,2},{4,5},{5,4},{6,7},{7,6},{8,9},{9,8},{10,11... | collective-permute-start | bytes 1769480 | tf_op jit(solution)/shard_map/ppermute | solution.py:66
  31.2 18.8 %collective-permute-done.3 = bf16[256,1152]{1,0:T(8,128)(2,1)S(1)} collective-permute-done((bf16[256,1152]{1,0:T(8,128)(2,1)S(1)}, bf16[256,1152]{1,0:T(8,128)(2,1)S(1)}, u32[]{:S(2)}, u32[]{:S(2)}) %collective-permute-start.3) | collective-permute-done | bytes 589856 | tf_op jit(solution)/shard_map/ppermute | solution.py:66
  50.0 0.0 collective-permute-done.4
  50.0 1.0 broadcast_select_fusion.3
  51.0 1.9 %collective-permute-start.5 = (bf16[256,1152]{1,0:T(8,128)(2,1)}, bf16[256,1152]{1,0:T(8,128)(2,1)}, u32[]{:S(2)}, u32[]{:S(2)}) collective-permute-start(bf16[256,1152]{1,0:T(8,128)(2,1)} %broadcast_select_fusion.3), channel_id=1, source_target_pairs={{14,766},{1,17},{30,14},{17,33},{46,30},{33,49},{62,46},{49,65},{7... | collective-permute-start | bytes 1769480 | tf_op jit(solution)/shard_map/ppermute | solution.py:66
  52.9 0.5 fusion.33
  53.4 0.0 copy-done.4
  53.4 1.4 %fusion.60 = f32[256,1152]{1,0:T(8,128)} fusion(bf16[256,1152]{1,0:T(8,128)(2,1)S(1)} %get-tuple-element.4, f32[256,256]{0,1:T(8,128)S(1)} %get-tuple-element.13, f32[]{:T(128)} %bitcast), kind=kOutput, calls=%fused_computation.97 | convolution fusion | flops 151650304 | bytes 2031620 | tf_op jit(solution)/shard_map/dot_general | solution.py:106
  54.8 0.0 collective-permute-done
  54.9 1.5 %collective-permute-start.1 = (bf16[256,1152]{1,0:T(8,128)(2,1)}, bf16[256,1152]{1,0:T(8,128)(2,1)}, u32[]{:S(2)}, u32[]{:S(2)}) collective-permute-start(bf16[256,1152]{1,0:T(8,128)(2,1)} %collective-permute-done), channel_id=1, source_target_pairs={{13,765},{2,18},{29,13},{18,34},{45,29},{34,50},{61,45},{50,66},{7... | collective-permute-start | bytes 1769480 | tf_op jit(solution)/shard_map/ppermute | solution.py:66
  56.3 0.0 copy-done.2
  56.3 1.4 %fusion.59 = f32[256,1152]{1,0:T(8,128)} fusion(bf16[256,1152]{1,0:T(8,128)(2,1)S(1)} %get-tuple-element.5, f32[256,256]{0,1:T(8,128)S(1)} %get-tuple-element.13, f32[]{:T(128)} %bitcast), kind=kOutput, calls=%fused_computation.96 | convolution fusion | flops 151650304 | bytes 2031620 | tf_op jit(solution)/shard_map/dot_general | solution.py:107
  57.7 26.3 %collective-permute-done.5 = bf16[256,1152]{1,0:T(8,128)(2,1)} collective-permute-done((bf16[256,1152]{1,0:T(8,128)(2,1)}, bf16[256,1152]{1,0:T(8,128)(2,1)}, u32[]{:S(2)}, u32[]{:S(2)}) %collective-permute-start.5) | collective-permute-done | bytes 589856 | tf_op jit(solution)/shard_map/ppermute | solution.py:66
  84.0 2.2 %broadcast_select_fusion = (bf16[256,1152]{1,0:T(8,128)(2,1)}, bf16[256,1152]{1,0:T(8,128)(2,1)}) fusion(bf16[256,1152]{1,0:T(8,128)(2,1)} %collective-permute-done.5, bf16[256,1152]{1,0:T(8,128)(2,1)S(1)} %collective-permute-done.3, pred[]{:T(512)S(6)} %and.32, bf16[256,1152]{1,0:T(8,128)(2,1)} %copy-done.4, pred[]{:T(512)S(6)} %and.31), kind=kLoop, calls=%fused_computation.53 | loop fusion | flops 589824 | bytes 2949122 | tf_op jit(solution)/shard_map/jit(_where)/select_n | solution.py:90
  86.2 2.0 %collective-permute-start.6 = (bf16[256,1152]{1,0:T(8,128)(2,1)}, bf16[256,1152]{1,0:T(8,128)(2,1)}, u32[]{:S(2)}, u32[]{:S(2)}) collective-permute-start(bf16[256,1152]{1,0:T(8,128)(2,1)} %get-tuple-element.7), channel_id=1, source_target_pairs={{0,1},{1,0},{2,3},{3,2},{4,5},{5,4},{6,7},{7,6},{8,9},{9,8},{10,11... | collective-permute-start | bytes 1769480 | tf_op jit(solution)/shard_map/ppermute | solution.py:66
  88.3 2.4 %collective-permute-start.7 = (bf16[256,1152]{1,0:T(8,128)(2,1)}, bf16[256,1152]{1,0:T(8,128)(2,1)}, u32[]{:S(2)}, u32[]{:S(2)}) collective-permute-start(bf16[256,1152]{1,0:T(8,128)(2,1)} %get-tuple-element.6), channel_id=1, source_target_pairs={{0,1},{1,0},{2,3},{3,2},{4,5},{5,4},{6,7},{7,6},{8,9},{9,8},{10,11... | collective-permute-start | bytes 1769480 | tf_op jit(solution)/shard_map/ppermute | solution.py:66
  90.7 0.0 collective-permute-done.1
  90.7 1.1 broadcast_select_fusion.2
  91.9 0.0 collective-permute-done.2
  91.9 0.0 copy-start.5
  91.9 1.7 %fusion.34 = (f32[256]{0:T(256)S(1)}, f32[256,256]{0,1:T(8,128)S(1)}) fusion(f32[]{:T(128)} %bitcast.26, bf16[256,1152]{1,0:T(8,128)(2,1)S(1)} %copy-done.3, bf16[256,1152]{1,0:T(8,128)(2,1)S(1)} %broadcast_select_fusion.2, bf16[256,1152]{1,0:T(8,128)(2,1)} %collective-permute-done.2, pred[]{:T(512)S(6)} %eq.30, f32[]{:T(128)} %bitcast), kind=kOutput, calls=%fused_computation.62 | convolution fusion | flops 151879424 | bytes 2032649 | tf_op jit(solution)/shard_map/dot_general | solution.py:100
  93.6 2.5 %convolution_add_fusion.3 = f32[256,1152]{1,0:T(8,128)} fusion(f32[256,1152]{1,0:T(8,128)S(1)} %copy-done.5, bf16[256,1152]{1,0:T(8,128)(2,1)S(1)} %broadcast_select_fusion.2, bf16[256,1152]{1,0:T(8,128)(2,1)} %collective-permute-done.2, pred[]{:T(512)S(6)} %eq.30, f32[256,256]{0,1:T(8,128)S(1)} %get-tuple-element.15, f32[]{:T(128)} %bitcast), kind=kOutput, calls=%fused_computation.3 | convolution fusion | flops 151912448 | bytes 3801093 | tf_op jit(solution)/shard_map/dot_general | solution.py:111
  96.1 2.8 %fusion.35 = (f32[256]{0:T(256)}, f32[256,256]{0,1:T(8,128)}) fusion(f32[]{:T(128)} %bitcast.25, bf16[256,1152]{1,0:T(8,128)(2,1)S(1)} %copy-done.3, bf16[256,1152]{1,0:T(8,128)(2,1)} %get-tuple-element.7, f32[]{:T(128)} %bitcast), kind=kOutput, calls=%fused_computation.63 | convolution fusion | flops 151584512 | bytes 1442824 | tf_op jit(solution)/shard_map/dot_general | solution.py:100
  98.9 3.2 %convolution_add_fusion.1 = f32[256,1152]{1,0:T(8,128)} fusion(f32[256,1152]{1,0:T(8,128)} %fusion.59, bf16[256,1152]{1,0:T(8,128)(2,1)S(1)} %get-tuple-element.4, bf16[256,1152]{1,0:T(8,128)(2,1)} %collective-permute-done.2, bf16[256,1152]{1,0:T(8,128)(2,1)S(1)} %broadcast_select_fusion.2, pred[]{:T(512)S(6)} %eq.30, f32[]{:T(128)} %bitcast.23, f32[]{:T(128)} %bitcast), kind=kOutput, calls=%fused_computation.1 | convolution fusion | flops 303333376 | bytes 4128777 | tf_op jit(solution)/shard_map/dot_general | solution.py:114
  102.1 0.0 collective-permute-done.6
  102.1 1.7 %fusion.36 = (f32[256]{0:T(256)S(1)}, f32[256,256]{0,1:T(8,128)S(1)}) fusion(f32[]{:T(128)} %bitcast.24, bf16[256,1152]{1,0:T(8,128)(2,1)} %copy-done.2, bf16[256,1152]{1,0:T(8,128)(2,1)} %collective-permute-done.6, f32[]{:T(128)} %bitcast), kind=kOutput, calls=%fused_computation.64 | convolution fusion | flops 151584512 | bytes 1442824 | tf_op jit(solution)/shard_map/dot_general | solution.py:100
  103.9 0.0 copy-start.6
  103.9 0.0 copy-start.8
  103.9 1.6 %fusion.37 = f32[256,1152]{1,0:T(8,128)S(1)} fusion(bf16[256,1152]{1,0:T(8,128)(2,1)} %collective-permute-done.6, f32[256,256]{0,1:T(8,128)S(1)} %get-tuple-element.9, f32[]{:T(128)} %bitcast), kind=kOutput, calls=%fused_computation.71 | convolution fusion | flops 151322624 | bytes 2031620 | tf_op jit(solution)/shard_map/dot_general | solution.py:111
  105.5 1.7 %multiply_reduce_fusion.1 = (f32[256]{0:T(256)S(1)}, f32[256,1152]{1,0:T(8,128)S(1)}) fusion(f32[256,1152]{1,0:T(8,128)S(1)} %copy-done, f32[256]{0:T(256)S(1)} %get-tuple-element.21, f32[256,1152]{1,0:T(8,128)S(1)} %fusion.37, f32[256,1152]{1,0:T(8,128)S(1)} %copy-done.6, bf16[256,1152]{1,0:T(8,128)(2,1)} %get-tuple-element.7, ...), kind=kOutput, calls=%fused_computation.9 | convolution fusion | flops 152796928 | bytes 5572612 | tf_op jit(solution)/shard_map/dot_general | solution.py:111
  107.1 1.3 %subtract_divide_fusion.1 = f32[256,1152]{1,0:T(8,128)} fusion(f32[256,1152]{1,0:T(8,128)S(1)} %get-tuple-element.17, f32[256]{0:T(256)S(1)} %get-tuple-element.16, f32[256]{0:T(256)S(1)} %get-tuple-element.21, f32[256,1152]{1,0:T(8,128)S(1)} %copy-done), kind=kLoop, calls=%fused_computation.8 | loop fusion | flops 1179648 | bytes 3540992 | tf_op jit(solution)/shard_map/div | solution.py:62
  108.4 0.0 collective-permute-done.7
  108.4 3.2 %fusion.28 = f32[256,1152]{1,0:T(8,128)} fusion(bf16[256,1152]{1,0:T(8,128)(2,1)} %collective-permute-done.7, bf16[256,1152]{1,0:T(8,128)(2,1)S(1)} %get-tuple-element.4, f32[]{:T(128)} %bitcast.21, f32[]{:T(128)} %bitcast), kind=kOutput, calls=%fused_computation.45 | convolution fusion | flops 302448640 | bytes 2359304 | tf_op jit(solution)/shard_map/dot_general | solution.py:114
  111.6 3.0 %multiply_reduce_fusion = (f32[256]{0:T(256)S(1)}, f32[256,1152]{1,0:T(8,128)S(1)}) fusion(f32[256,1152]{1,0:T(8,128)S(1)} %copy-done.1, f32[256]{0:T(256)S(1)} %get-tuple-element.20, f32[256,1152]{1,0:T(8,128)} %fusion.28, f32[256,1152]{1,0:T(8,128)} %convolution_add_fusion.1, bf16[256,1152]{1,0:T(8,128)(2,1)} %get-tuple-element.6, ...), kind=kOutput, calls=%fused_computation.7 | convolution fusion | flops 303922944 | bytes 5900296 | tf_op jit(solution)/shard_map/dot_general | solution.py:114
  114.6 0.0 copy-start.7
  114.6 1.3 %subtract_divide_fusion = f32[256,1152]{1,0:T(8,128)} fusion(f32[256,1152]{1,0:T(8,128)S(1)} %get-tuple-element.19, f32[256]{0:T(256)S(1)} %get-tuple-element.18, f32[256]{0:T(256)S(1)} %get-tuple-element.20, f32[256,1152]{1,0:T(8,128)S(1)} %copy-done.1), kind=kLoop, calls=%fused_computation.6 | loop fusion | flops 1179648 | bytes 3540992 | tf_op jit(solution)/shard_map/div | solution.py:62
  115.9 0.6 add_multiply_fusion
  (9 shorter events, 0.0 us)
Async XLA Ops:
  0.6 1.6 %copy-start = (f32[256,1152]{1,0:T(8,128)S(1)}, f32[256,1152]{1,0:T(8,128)}, u32[]{:S(2)}) copy-start(f32[256,1152]{1,0:T(8,128)} %param.4) | copy-start | bytes 3538948
  0.7 2.0 %copy-start.1 = (f32[256,1152]{1,0:T(8,128)S(1)}, f32[256,1152]{1,0:T(8,128)}, u32[]{:S(2)}) copy-start(f32[256,1152]{1,0:T(8,128)} %param.5) | copy-start | bytes 3538948
  3.8 52.6 %copy-start.2 = (bf16[256,1152]{1,0:T(8,128)(2,1)}, bf16[256,1152]{1,0:T(8,128)(2,1)S(1)}, u32[]{:S(2)}) copy-start(bf16[256,1152]{1,0:T(8,128)(2,1)S(1)} %get-tuple-element.5) | copy-start | bytes 1769476
  3.8 46.3 %collective-permute-start.3 = (bf16[256,1152]{1,0:T(8,128)(2,1)S(1)}, bf16[256,1152]{1,0:T(8,128)(2,1)S(1)}, u32[]{:S(2)}, u32[]{:S(2)}) collective-permute-start(bf16[256,1152]{1,0:T(8,128)(2,1)S(1)} %get-tuple-element.5), channel_id=1, source_target_pairs={{0,14},{1,767},{2,0},{3,1},{4,2},{5,3},{6,4},{7,5},{8,6},{9,7},{10... | collective-permute-start | bytes 1769480 | tf_op jit(solution)/shard_map/ppermute | solution.py:66
  24.0 26.0 %collective-permute-start.4 = (bf16[256,1152]{1,0:T(8,128)(2,1)S(1)}, bf16[256,1152]{1,0:T(8,128)(2,1)S(1)}, u32[]{:S(2)}, u32[]{:S(2)}) collective-permute-start(bf16[256,1152]{1,0:T(8,128)(2,1)S(1)} %get-tuple-element.4), channel_id=1, source_target_pairs={{0,2},{1,3},{2,4},{3,5},{4,6},{5,7},{6,8},{7,9},{8,10},{9,11},{10,... | collective-permute-start | bytes 1769480 | tf_op jit(solution)/shard_map/ppermute | solution.py:66
  26.0 28.9 %collective-permute-start = (bf16[256,1152]{1,0:T(8,128)(2,1)S(1)}, bf16[256,1152]{1,0:T(8,128)(2,1)}, u32[]{:S(2)}, u32[]{:S(2)}) collective-permute-start(bf16[256,1152]{1,0:T(8,128)(2,1)S(1)} %broadcast_select_fusion.6), channel_id=1, source_target_pairs={{0,13},{1,4},{2,767},{3,6},{4,1},{5,8},{6,3},{7,10},{8,5},{9,12},{... | collective-permute-start | bytes 1769480 | tf_op jit(solution)/shard_map/ppermute | solution.py:66
  27.9 63.9 %collective-permute-start.2 = (bf16[256,1152]{1,0:T(8,128)(2,1)}, bf16[256,1152]{1,0:T(8,128)(2,1)}, u32[]{:S(2)}, u32[]{:S(2)}) collective-permute-start(bf16[256,1152]{1,0:T(8,128)(2,1)} %get-tuple-element.3), channel_id=1, source_target_pairs={{0,1},{1,0},{2,3},{3,2},{4,5},{5,4},{6,7},{7,6},{8,9},{9,8},{10,11... | collective-permute-start | bytes 1769480 | tf_op jit(solution)/shard_map/ppermute | solution.py:66
  50.0 3.4 %copy-start.4 = (bf16[256,1152]{1,0:T(8,128)(2,1)}, bf16[256,1152]{1,0:T(8,128)(2,1)S(1)}, u32[]{:S(2)}) copy-start(bf16[256,1152]{1,0:T(8,128)(2,1)S(1)} %collective-permute-done.4) | copy-start | bytes 1769476
  51.0 33.1 %collective-permute-start.5 = (bf16[256,1152]{1,0:T(8,128)(2,1)}, bf16[256,1152]{1,0:T(8,128)(2,1)}, u32[]{:S(2)}, u32[]{:S(2)}) collective-permute-start(bf16[256,1152]{1,0:T(8,128)(2,1)} %broadcast_select_fusion.3), channel_id=1, source_target_pairs={{14,766},{1,17},{30,14},{17,33},{46,30},{33,49},{62,46},{49,65},{7... | collective-permute-start | bytes 1769480 | tf_op jit(solution)/shard_map/ppermute | solution.py:66
  54.9 35.9 %collective-permute-start.1 = (bf16[256,1152]{1,0:T(8,128)(2,1)}, bf16[256,1152]{1,0:T(8,128)(2,1)}, u32[]{:S(2)}, u32[]{:S(2)}) collective-permute-start(bf16[256,1152]{1,0:T(8,128)(2,1)} %collective-permute-done), channel_id=1, source_target_pairs={{13,765},{2,18},{29,13},{18,34},{45,29},{34,50},{61,45},{50,66},{7... | collective-permute-start | bytes 1769480 | tf_op jit(solution)/shard_map/ppermute | solution.py:66
  86.2 5.6 %copy-start.3 = (bf16[256,1152]{1,0:T(8,128)(2,1)S(1)}, bf16[256,1152]{1,0:T(8,128)(2,1)}, u32[]{:S(2)}) copy-start(bf16[256,1152]{1,0:T(8,128)(2,1)} %copy-done.2) | copy-start | bytes 1769476
  86.2 15.9 %collective-permute-start.6 = (bf16[256,1152]{1,0:T(8,128)(2,1)}, bf16[256,1152]{1,0:T(8,128)(2,1)}, u32[]{:S(2)}, u32[]{:S(2)}) collective-permute-start(bf16[256,1152]{1,0:T(8,128)(2,1)} %get-tuple-element.7), channel_id=1, source_target_pairs={{0,1},{1,0},{2,3},{3,2},{4,5},{5,4},{6,7},{7,6},{8,9},{9,8},{10,11... | collective-permute-start | bytes 1769480 | tf_op jit(solution)/shard_map/ppermute | solution.py:66
  88.3 20.2 %collective-permute-start.7 = (bf16[256,1152]{1,0:T(8,128)(2,1)}, bf16[256,1152]{1,0:T(8,128)(2,1)}, u32[]{:S(2)}, u32[]{:S(2)}) collective-permute-start(bf16[256,1152]{1,0:T(8,128)(2,1)} %get-tuple-element.6), channel_id=1, source_target_pairs={{0,1},{1,0},{2,3},{3,2},{4,5},{5,4},{6,7},{7,6},{8,9},{9,8},{10,11... | collective-permute-start | bytes 1769480 | tf_op jit(solution)/shard_map/ppermute | solution.py:66
  91.9 1.7 %copy-start.5 = (f32[256,1152]{1,0:T(8,128)S(1)}, f32[256,1152]{1,0:T(8,128)}, u32[]{:S(2)}) copy-start(f32[256,1152]{1,0:T(8,128)} %fusion.60) | copy-start | bytes 3538948
  103.9 1.6 %copy-start.6 = (f32[256,1152]{1,0:T(8,128)S(1)}, f32[256,1152]{1,0:T(8,128)}, u32[]{:S(2)}) copy-start(f32[256,1152]{1,0:T(8,128)} %convolution_add_fusion.3) | copy-start | bytes 3538948
  103.9 1.6 %copy-start.8 = (f32[256,256]{0,1:T(8,128)S(1)}, f32[256,256]{0,1:T(8,128)}, u32[]{:S(2)}) copy-start(f32[256,256]{0,1:T(8,128)} %get-tuple-element.11) | copy-start | bytes 786436
  114.6 1.3 %copy-start.7 = (f32[256]{0:T(256)S(1)}, f32[256]{0:T(256)}, u32[]{:S(2)}) copy-start(f32[256]{0:T(256)} %get-tuple-element.10) | copy-start | bytes 3076

commit v2 on v0

v2 whole, which is shorter than its diff:
```python
import functools

import jax
import jax.numpy as jnp
from jax import lax
from jax.experimental import pallas as pl
from jax.experimental.pallas import tpu as pltpu
from jax.sharding import PartitionSpec as P

BAND = 4
AXES = ("dp", "rows")
X, Y, Z, CORES = 4, 8, 12, 2
COUNT = X * Y * Z * CORES
Z_LO, Z_HI = 4, 3
HALF = jnp.bfloat16
WIDE = jnp.float32
PIECE = 64
LANES = 384


def place(k):
    core = k % CORES
    y = (k // CORES) % Y
    z_hi = (k // (CORES * Y)) % Z_HI
    x = (k // (CORES * Y * Z_HI)) % X
    z_lo = k // (CORES * Y * Z_HI * X)
    return x, y, z_hi * Z_LO + z_lo, core


INDEX = {place(k): k for k in range(COUNT)}


def routes():
    near, across, turned, far, far_turned, swap, pass_near, pass_turned = [], [], [], [], [], [], [], []
    for k in range(COUNT):
        x, y, z, core = place(k)
        edge = 7 if core == 1 else 0
        way = 1 if core == 1 else -1
        one, two, three = (k + way) % COUNT, (k + 2 * way) % COUNT, (k + 3 * way) % COUNT
        swap.append((k, k ^ 1))
        across.append((k, (k - 2 * way) % COUNT))
        if y == edge:
            stop = INDEX[(x, 7 - edge, z, core)]
            near.append((k, stop))
            turned.append((stop, two))
        else:
            near.append((k, two))
            if y != 7 - edge:
                far.append((k, one))
        if y == edge - way:
            turned.append((k, three))
        if y == 7 - edge:
            pass_turned.append((k, k ^ 1))
            far_turned.append((k, one))
        else:
            pass_near.append((k, k ^ 1))
    return near, across, turned, far, far_turned, swap, pass_near, pass_turned


def send(value, pairs):
    return lax.ppermute(value, AXES, pairs)


def rows_place():
    at = lax.axis_index("rows")
    return at % CORES, (at // CORES) % Y


def fetch(first, one, two, wide, sems, swap):
    count = wide.shape[0]

    def start(source):
        for i in range(count // PIECE):
            rows = pl.ds(i * PIECE, PIECE)
            pltpu.make_async_copy(source.at[rows], wide.at[rows], sems.at[i]).start()

    @pl.when(first != swap)
    def _():
        start(one)

    @pl.when(first == swap)
    def _():
        start(two)


def arrived(i, one, wide, sems):
    rows = pl.ds(i * PIECE, PIECE)
    pltpu.make_async_copy(one.at[rows], wide.at[rows], sems.at[i]).wait()
    return rows


def unit_kernel(swap, images, texts, half, norm, wide, sems):
    core, _ = rows_place()
    fetch(core == 0, images, texts, wide, sems, swap)
    for i in range(wide.shape[0] // PIECE):
        rows = arrived(i, images, wide, sems)
        values = wide[rows]
        size = jnp.sqrt(jnp.sum(values * values, axis=-1, keepdims=True) + 1e-06)
        norm[rows] = size
        half[rows] = (values / size).astype(HALF)


def tile(consts, own, other, diagonal, loss, logits, dlogit):
    scale, shift_b = jnp.exp(consts[0]), consts[1]
    logits[...] = lax.dot_general(own[...], other[...], (((1,), (1,)), ((), ())), preferred_element_type=WIDE)
    for i in range(logits.shape[0] // PIECE):
        rows = pl.ds(i * PIECE, PIECE)
        value = scale * logits[rows] + shift_b
        if diagonal:
            shape = value.shape
            same = lax.broadcasted_iota(jnp.int32, shape, 0) + i * PIECE == lax.broadcasted_iota(jnp.int32, shape, 1)
            value = jnp.where(same, -value, value)
        small = jnp.exp(-jnp.abs(value))
        loss[rows] += jnp.sum(jnp.maximum(value, 0.0) + jnp.log1p(small), axis=-1, keepdims=True)
        grad = jnp.where(value >= 0, 1.0, small) / (1.0 + small) * scale
        if diagonal:
            grad = jnp.where(same, -grad, grad)
        dlogit[rows] = grad.astype(HALF)


def add_grad(grad, dlogit, other, fresh=False):
    for i in range(grad.shape[1] // LANES):
        cols = pl.ds(i * LANES, LANES)
        part = jnp.dot(dlogit[...], other[:, cols], preferred_element_type=WIDE)
        grad[:, cols] = part if fresh else grad[:, cols] + part


def first_kernel(consts, u, v, beside, across, passed, grad_u, grad_v, loss_u, loss_v, logits, dlogit):
    loss_u[...] = jnp.zeros_like(loss_u)
    loss_v[...] = jnp.zeros_like(loss_v)
    for own, grad, loss, others in ((u, grad_u, loss_u, (v, across)), (v, grad_v, loss_v, (u, beside, passed))):
        for i, other in enumerate(others):
            tile(consts, own, other, i == 0, loss, logits, dlogit)
            add_grad(grad, dlogit, other, i == 0)


def back(rows, values, norm, grad):
    size = norm[rows]
    unit = values / size
    value = grad[rows]
    along = jnp.sum(unit * value, axis=-1, keepdims=True)
    return (value - unit * along) / size


def second_kernel(consts, v, near, turned, images, texts, norm_v, grad_v_in, loss_v_in, grad_v, loss_v,
                  logits, dlogit, block, wide, sems):
    core, y = rows_place()
    fetch(core == 0, images, texts, wide, sems, True)
    edge = jnp.where(core == 0, 7, 0)
    loss_v[...] = loss_v_in[...]
    grad_v[...] = grad_v_in[...]
    block[...] = jnp.where(y == edge, turned[...], near[...])
    tile(consts, v, block, False, loss_v, logits, dlogit)
    add_grad(grad_v, dlogit, block)
    for i in range(wide.shape[0] // PIECE):
        rows = arrived(i, images, wide, sems)
        grad_v[rows] = back(rows, wide[rows], norm_v, grad_v)


def last_kernel(consts, u, passed, passed_turned, far, leap, far_turned, images, texts, norm_u, grad_u_in, grad_v, loss_u_in,
                loss_v, row_loss, image_grad, text_grad, grad_u, loss_u, logits, dlogit, block, wide, sems, out_sems, v_sem):
    core, y = rows_place()
    count = wide.shape[0]
    pieces = count // PIECE
    fetch(core == 0, images, texts, wide, sems, False)

    @pl.when(core == 0)
    def _():
        pltpu.make_async_copy(grad_v, text_grad, v_sem).start()

    @pl.when(core != 0)
    def _():
        pltpu.make_async_copy(grad_v, image_grad, v_sem).start()

    edge, after = jnp.where(core == 0, 0, 7), jnp.where(core == 0, 1, 6)
    loss_u[...] = loss_u_in[...]
    grad_u[...] = grad_u_in[...]
    block[...] = jnp.where(y == edge, passed_turned[...], passed[...])
    tile(consts, u, block, False, loss_u, logits, dlogit)
    add_grad(grad_u, dlogit, block)
    block[...] = jnp.where(y == edge, leap[...], jnp.where(y == after, far_turned[...], far[...]))
    tile(consts, u, block, False, loss_u, logits, dlogit)
    add_grad(grad_u, dlogit, block)
    for i in range(pieces):
        rows = arrived(i, images, wide, sems)
        grad_u[rows] = back(rows, wide[rows], norm_u, grad_u)

        @pl.when(core == 0)
        def _():
            pltpu.make_async_copy(grad_u.at[rows], image_grad.at[rows], out_sems.at[i]).start()

        @pl.when(core != 0)
        def _():
            pltpu.make_async_copy(grad_u.at[rows], text_grad.at[rows], out_sems.at[i]).start()

    total = jnp.where(core == 0, loss_u[...], loss_v[...]) / (BAND * count)
    row_loss[...] = jnp.broadcast_to(total, (count, 128)).T[0:1]
    for i in range(pieces):
        rows = pl.ds(i * PIECE, PIECE)
        pltpu.make_async_copy(grad_u.at[rows], image_grad.at[rows], out_sems.at[i]).wait()
    pltpu.make_async_copy(grad_v, text_grad, v_sem).wait()


VMEM = pl.BlockSpec(memory_space=pltpu.VMEM)
SMEM = pl.BlockSpec(memory_space=pltpu.SMEM)
HBM = pl.BlockSpec(memory_space=pltpu.HBM)
PARAMS = pltpu.CompilerParams(vmem_limit_bytes=24 * 2**20)


def cost(tiles):
    return pl.CostEstimate(flops=tiles * 40 * 256 * 256 * 1152, bytes_accessed=4 * 2**20, transcendentals=0)


def local(images, texts, log_temp, bias):
    near_to, across_to, turned_to, far_to, far_turned_to, swap_to, pass_near_to, pass_turned_to = routes()
    count, width = images.shape
    pieces = count // PIECE
    consts = jnp.concatenate([log_temp, bias])
    half = jax.ShapeDtypeStruct((count, width), HALF)
    wide = jax.ShapeDtypeStruct((count, width), WIDE)
    column = jax.ShapeDtypeStruct((count, 1), WIDE)
    logits = pltpu.VMEM((count, count), WIDE)
    dlogit = pltpu.VMEM((count, count), HALF)
    half_room = pltpu.VMEM((count, width), HALF)
    wide_room = pltpu.VMEM((count, width), WIDE)
    column_room = pltpu.VMEM((count, 1), WIDE)
    sems = pltpu.SemaphoreType.DMA((pieces,))

    def unit(swap):
        return pl.pallas_call(
            functools.partial(unit_kernel, swap),
            out_shape=(half, column),
            in_specs=[HBM, HBM],
            out_specs=(VMEM, VMEM),
            scratch_shapes=[wide_room, sems],
            compiler_params=PARAMS,
        )(images, texts)

    _, y = rows_place()
    u, norm_u = unit(False)
    near = send(u, near_to)
    v, norm_v = unit(True)
    across = send(v, across_to)
    turned = send(jnp.where((y == 0) | (y == 7), near, u), turned_to)
    beside = send(v, swap_to)
    far = send(near, far_to)
    passed_near = send(near, pass_near_to)
    passed_across = send(across, swap_to)
    far_turned = send(turned, far_turned_to)
    passed_turned = send(turned, pass_turned_to)

    grad_u, grad_v, loss_u, loss_v = pl.pallas_call(
        first_kernel,
        out_shape=(wide, wide, column, column),
        in_specs=[SMEM] + [VMEM] * 5,
        out_specs=(VMEM,) * 4,
        scratch_shapes=[logits, dlogit],
        compiler_params=PARAMS,
        cost_estimate=cost(5),
    )(consts, u, v, beside, across, passed_across)
    grad_v, loss_v = pl.pallas_call(
        second_kernel,
        out_shape=(wide, column),
        in_specs=[SMEM] + [VMEM] * 3 + [HBM] * 2 + [VMEM] * 3,
        out_specs=(VMEM,) * 2,
        scratch_shapes=[logits, dlogit, half_room, wide_room, sems],
        compiler_params=PARAMS,
        cost_estimate=cost(1),
    )(consts, v, near, turned, images, texts, norm_v, grad_v, loss_v)
    row_loss, image_grad, text_grad = pl.pallas_call(
        last_kernel,
        out_shape=(jax.ShapeDtypeStruct((1, count), WIDE), wide, wide),
        in_specs=[SMEM] + [VMEM] * 6 + [HBM] * 2 + [VMEM] * 5,
        out_specs=(VMEM, HBM, HBM),
        scratch_shapes=[wide_room, column_room, logits, dlogit, half_room, wide_room, sems, sems, pltpu.SemaphoreType.DMA],
        compiler_params=PARAMS,
        cost_estimate=cost(2),
    )(consts, u, passed_near, passed_turned, far, turned, far_turned, images, texts, norm_u, grad_u, grad_v, loss_u, loss_v)
    return (row_loss.reshape(count), image_grad, text_grad)


def solution(mesh):
    placed = (P(AXES, None), P(AXES, None), P(), P())
    return jax.shard_map(
        local,
        mesh=mesh,
        in_specs=placed,
        out_specs=(P(AXES), P(AXES, None), P(AXES, None)),
        check_vma=False,
    )
```

time: 320 us -> 80.6 us (0.25)
  the two profiles are of different devices: /device:TPU:64 before, /device:TPU:1 now
where the time goes in v2:
time: 80.6 us; the launch traced here: 79.2 us
  starting transfers between devices  38.9 us (48%)
  waiting for transfers between devices  21.8 us (27%)
  Pallas kernels  13.6 us (17%)
  local copies, waits for them, and re-layouts  2.54 us (3%)
  between operations  2.17 us (3%)
    ppermute x9, starting transfers between devices, send(): return lax.ppermute(value, AXES, pairs)  38.9 us
    ppermute x9, waiting for transfers between devices, send(): return lax.ppermute(value, AXES, pairs)  21.8 us
    pallas_call x1, Pallas kernels, local(): pl.pallas_call(last_kernel, out_shape=(jax.ShapeDtypeStruct((1, count), W...  4.62 us
    pallas_call x1, Pallas kernels, local(): pl.pallas_call(first_kernel, out_shape=(wide, wide, column, column), in_s...  4.53 us
    pallas_call x1, Pallas kernels, local(): pl.pallas_call(second_kernel, out_shape=(wide, column), in_specs=[SMEM] +...  2.8 us
    unnamed x8, local copies, waits for them, and re-layouts  2.54 us
    pallas_call x2, Pallas kernels, unit(): pl.pallas_call(functools.partial(unit_kernel, swap), out_shape=(half, col...  1.63 us
  transfers between devices with their start and end apart: 9, of which 1 were waited for; matrix products, arithmetic and copies ran while one was open for 0% of the time, Pallas kernels for 10%

profile of v2, /device:TPU:1, one launch (start us, length us, event | category | flops | bytes accessed | tf_op | source)
XLA Modules:
  0.0 79.2 jit_solution(512847325677871009)
XLA Ops:
  0.6 0.0 copy-start
  0.6 1.3 %copy-done = f32[256,1152]{1,0:T(8,128)S(1)} copy-done((f32[256,1152]{1,0:T(8,128)S(1)}, f32[256,1152]{1,0:T(8,128)}, u32[]{:S(2)}) %copy-start) | copy-done | bytes 1179672
  1.9 0.0 copy-start.2
  1.9 1.3 %copy-done.2 = f32[256,1152]{1,0:T(8,128)S(1)} copy-done((f32[256,1152]{1,0:T(8,128)S(1)}, f32[256,1152]{1,0:T(8,128)}, u32[]{:S(2)}) %copy-start.2) | copy-done | bytes 1179672
  3.2 0.8 %shard_map.67 = (bf16[256,1152]{1,0:T(8,128)(2,1)S(1)}, f32[256,1]{1,0:T(8,128)S(1)}) custom-call(f32[256,1152]{1,0:T(8,128)S(1)} %copy-done, f32[256,1152]{1,0:T(8,128)S(1)} %copy-done.2), custom_call_target="tpu_custom_call" | custom-call | tf_op jit(solution)/shard_map/pallas_call | solution.py:230
  4.0 4.0 %collective-permute-start = (bf16[256,1152]{1,0:T(8,128)(2,1)S(1)}, bf16[256,1152]{1,0:T(8,128)(2,1)S(1)}, u32[]{:S(2)}, u32[]{:S(2)}) collective-permute-start(bf16[256,1152]{1,0:T(8,128)(2,1)S(1)} %get-tuple-element.16.u), channel_id=1, source_target_pairs={{0,14},{1,3},{2,0},{3,5},{4,2},{5,7},{6,4},{7,9},{8,6},{9,11},{10,... | collective-permute-start | bytes 1769480 | tf_op jit(solution)/shard_map/ppermute | solution.py:61
  8.0 0.8 %shard_map.68 = (bf16[256,1152]{1,0:T(8,128)(2,1)S(1)}, f32[256,1]{1,0:T(8,128)S(1)}) custom-call(f32[256,1152]{1,0:T(8,128)S(1)} %copy-done, f32[256,1152]{1,0:T(8,128)S(1)} %copy-done.2), custom_call_target="tpu_custom_call" | custom-call | tf_op jit(solution)/shard_map/pallas_call | solution.py:230
  8.9 18.1 %collective-permute-start.7 = (bf16[256,1152]{1,0:T(8,128)(2,1)S(1)}, bf16[256,1152]{1,0:T(8,128)(2,1)S(1)}, u32[]{:S(2)}, u32[]{:S(2)}) collective-permute-start(bf16[256,1152]{1,0:T(8,128)(2,1)S(1)} %get-tuple-element.18.v), channel_id=1, source_target_pairs={{0,2},{1,767},{2,4},{3,1},{4,6},{5,3},{6,8},{7,5},{8,10},{9,7},{10... | collective-permute-start | bytes 1769480 | tf_op jit(solution)/shard_map/ppermute | solution.py:61
  27.0 0.0 collective-permute-done.near
  27.1 0.1 broadcast_select_fusion
  27.1 1.9 %collective-permute-start.2 = (bf16[256,1152]{1,0:T(8,128)(2,1)S(1)}, bf16[256,1152]{1,0:T(8,128)(2,1)S(1)}, u32[]{:S(2)}, u32[]{:S(2)}) collective-permute-start(bf16[256,1152]{1,0:T(8,128)(2,1)S(1)} %broadcast_select_fusion), channel_id=1, source_target_pairs={{14,766},{2,767},{13,16},{1,17},{30,14},{18,15},{29,32},{17,33},{4... | collective-permute-start | bytes 1769480 | tf_op jit(solution)/shard_map/ppermute | solution.py:61
  29.1 1.9 %collective-permute-start.6 = (bf16[256,1152]{1,0:T(8,128)(2,1)S(1)}, bf16[256,1152]{1,0:T(8,128)(2,1)S(1)}, u32[]{:S(2)}, u32[]{:S(2)}) collective-permute-start(bf16[256,1152]{1,0:T(8,128)(2,1)S(1)} %get-tuple-element.18.v), channel_id=1, source_target_pairs={{0,1},{1,0},{2,3},{3,2},{4,5},{5,4},{6,7},{7,6},{8,9},{9,8},{10,11... | collective-permute-start | bytes 1769480 | tf_op jit(solution)/shard_map/ppermute | solution.py:61
  31.0 21.8 %collective-permute-done.7.across = bf16[256,1152]{1,0:T(8,128)(2,1)S(1)} collective-permute-done((bf16[256,1152]{1,0:T(8,128)(2,1)S(1)}, bf16[256,1152]{1,0:T(8,128)(2,1)S(1)}, u32[]{:S(2)}, u32[]{:S(2)}) %collective-permute-start.7) | collective-permute-done | bytes 589856 | tf_op jit(solution)/shard_map/ppermute | solution.py:61
  52.8 5.2 %collective-permute-start.8 = (bf16[256,1152]{1,0:T(8,128)(2,1)S(1)}, bf16[256,1152]{1,0:T(8,128)(2,1)S(1)}, u32[]{:S(2)}, u32[]{:S(2)}) collective-permute-start(bf16[256,1152]{1,0:T(8,128)(2,1)S(1)} %collective-permute-done.7.across), channel_id=1, source_target_pairs={{0,1},{1,0},{2,3},{3,2},{4,5},{5,4},{6,7},{7,6},{8,9},{9,8},{10,11... | collective-permute-start | bytes 1769480 | tf_op jit(solution)/shard_map/ppermute | solution.py:61
  59.3 0.1 pad_maximum_fusion.consts
  59.3 0.0 copy-start.1
  59.3 0.0 copy-start.3
  59.3 1.4 %collective-permute-start.1 = (bf16[256,1152]{1,0:T(8,128)(2,1)S(1)}, bf16[256,1152]{1,0:T(8,128)(2,1)S(1)}, u32[]{:S(2)}, u32[]{:S(2)}) collective-permute-start(bf16[256,1152]{1,0:T(8,128)(2,1)S(1)} %collective-permute-done.near), channel_id=1, source_target_pairs={{0,1},{2,3},{3,2},{4,5},{5,4},{6,7},{7,6},{8,9},{9,8},{10,11},{11,... | collective-permute-start | bytes 1769480 | tf_op jit(solution)/shard_map/ppermute | solution.py:61
  60.8 1.3 %collective-permute-start.4 = (bf16[256,1152]{1,0:T(8,128)(2,1)S(1)}, bf16[256,1152]{1,0:T(8,128)(2,1)S(1)}, u32[]{:S(2)}, u32[]{:S(2)}) collective-permute-start(bf16[256,1152]{1,0:T(8,128)(2,1)S(1)} %collective-permute-done.near), channel_id=1, source_target_pairs={{2,1},{3,4},{4,3},{5,6},{6,5},{7,8},{8,7},{9,10},{10,9},{11,12},{1... | collective-permute-start | bytes 1769480 | tf_op jit(solution)/shard_map/ppermute | solution.py:61
  62.1 0.0 collective-permute-done.2.turned.leap
  62.1 3.2 %collective-permute-start.3 = (bf16[256,1152]{1,0:T(8,128)(2,1)S(1)}, bf16[256,1152]{1,0:T(8,128)(2,1)S(1)}, u32[]{:S(2)}, u32[]{:S(2)}) collective-permute-start(bf16[256,1152]{1,0:T(8,128)(2,1)S(1)} %collective-permute-done.2.turned.leap), channel_id=1, source_target_pairs={{1,0},{14,15},{17,16},{30,31},{33,32},{46,47},{49,48},{62,63},{65,... | collective-permute-start | bytes 1769480 | tf_op jit(solution)/shard_map/ppermute | solution.py:61
  65.2 0.0 collective-permute-done.6.beside
  65.2 1.9 %collective-permute-start.5 = (bf16[256,1152]{1,0:T(8,128)(2,1)S(1)}, bf16[256,1152]{1,0:T(8,128)(2,1)S(1)}, u32[]{:S(2)}, u32[]{:S(2)}) collective-permute-start(bf16[256,1152]{1,0:T(8,128)(2,1)S(1)} %collective-permute-done.2.turned.leap), channel_id=1, source_target_pairs={{1,2},{14,13},{17,18},{30,29},{33,34},{46,45},{49,50},{62,61},{65,... | collective-permute-start | bytes 1769480 | tf_op jit(solution)/shard_map/ppermute | solution.py:61
  67.1 0.0 collective-permute-done.8.passed
  67.1 4.5 %shard_map.69 = (f32[256,1152]{1,0:T(8,128)S(1)}, f32[256,1152]{1,0:T(8,128)S(1)}, f32[256,1]{1,0:T(8,128)S(1)}, f32[256,1]{1,0:T(8,128)S(1)}) custom-call(f32[2]{0:T(128)S(1)} %pad_maximum_fusion.consts, bf16[256,1152]{1,0:T(8,128)(2,1)S(1)} %get-tuple-element.16.u, bf16[256,1152]{1,0:T(8,128)(2,1)S(1)} %get-tuple-element.18.v, ...), custom_call_target="tpu_custom_call" | custom-call | flops 15099494400 | bytes 4194304 | tf_op jit(solution)/shard_map/pallas_call | solution.py:252
  71.7 0.0 copy-done.1
  71.7 0.0 copy-done.3
  71.7 2.8 %shard_map.70 = (f32[256,1152]{1,0:T(8,128)S(1)}, f32[256,1]{1,0:T(8,128)S(1)}) custom-call(f32[2]{0:T(128)S(1)} %pad_maximum_fusion.consts, bf16[256,1152]{1,0:T(8,128)(2,1)S(1)} %get-tuple-element.18.v, bf16[256,1152]{1,0:T(8,128)(2,1)S(1)} %collective-permute-done.near, bf16[256,1152]{1,0:T(8,128)(2,1)S(1)} %collective-permute-done.2.turned.leap, ...), custom_call_target="tpu_custom_call" | custom-call | flops 3019898880 | bytes 4194304 | tf_op jit(solution)/shard_map/pallas_call | solution.py:261
  74.5 0.0 collective-permute-done.1.passed
  74.5 0.0 collective-permute-done.4.far
  74.5 0.0 collective-permute-done.3.passed_turned
  74.5 0.0 collective-permute-done.5.far_turned
  74.6 4.6 %shard_map.71 = (f32[1,256]{1,0:T(1,128)}, f32[256,1152]{1,0:T(8,128)}, f32[256,1152]{1,0:T(8,128)}) custom-call(f32[2]{0:T(128)S(1)} %pad_maximum_fusion.consts, bf16[256,1152]{1,0:T(8,128)(2,1)S(1)} %get-tuple-element.16.u, bf16[256,1152]{1,0:T(8,128)(2,1)S(1)} %collective-permute-done.1.passed, ...), custom_call_target="tpu_custom_call" | custom-call | flops 6039797760 | bytes 4194304 | tf_op jit(solution)/shard_map/pallas_call | solution.py:270
Async XLA Ops:
  0.6 1.3 %copy-start = (f32[256,1152]{1,0:T(8,128)S(1)}, f32[256,1152]{1,0:T(8,128)}, u32[]{:S(2)}) copy-start(f32[256,1152]{1,0:T(8,128)} %images.7) | copy-start | bytes 3538948
  1.9 1.3 %copy-start.2 = (f32[256,1152]{1,0:T(8,128)S(1)}, f32[256,1152]{1,0:T(8,128)}, u32[]{:S(2)}) copy-start(f32[256,1152]{1,0:T(8,128)} %texts.7) | copy-start | bytes 3538948
  4.0 23.1 %collective-permute-start = (bf16[256,1152]{1,0:T(8,128)(2,1)S(1)}, bf16[256,1152]{1,0:T(8,128)(2,1)S(1)}, u32[]{:S(2)}, u32[]{:S(2)}) collective-permute-start(bf16[256,1152]{1,0:T(8,128)(2,1)S(1)} %get-tuple-element.16.u), channel_id=1, source_target_pairs={{0,14},{1,3},{2,0},{3,5},{4,2},{5,7},{6,4},{7,9},{8,6},{9,11},{10,... | collective-permute-start | bytes 1769480 | tf_op jit(solution)/shard_map/ppermute | solution.py:61
  8.9 43.9 %collective-permute-start.7 = (bf16[256,1152]{1,0:T(8,128)(2,1)S(1)}, bf16[256,1152]{1,0:T(8,128)(2,1)S(1)}, u32[]{:S(2)}, u32[]{:S(2)}) collective-permute-start(bf16[256,1152]{1,0:T(8,128)(2,1)S(1)} %get-tuple-element.18.v), channel_id=1, source_target_pairs={{0,2},{1,767},{2,4},{3,1},{4,6},{5,3},{6,8},{7,5},{8,10},{9,7},{10... | collective-permute-start | bytes 1769480 | tf_op jit(solution)/shard_map/ppermute | solution.py:61
  27.1 34.9 %collective-permute-start.2 = (bf16[256,1152]{1,0:T(8,128)(2,1)S(1)}, bf16[256,1152]{1,0:T(8,128)(2,1)S(1)}, u32[]{:S(2)}, u32[]{:S(2)}) collective-permute-start(bf16[256,1152]{1,0:T(8,128)(2,1)S(1)} %broadcast_select_fusion), channel_id=1, source_target_pairs={{14,766},{2,767},{13,16},{1,17},{30,14},{18,15},{29,32},{17,33},{4... | collective-permute-start | bytes 1769480 | tf_op jit(solution)/shard_map/ppermute | solution.py:61
  29.1 36.2 %collective-permute-start.6 = (bf16[256,1152]{1,0:T(8,128)(2,1)S(1)}, bf16[256,1152]{1,0:T(8,128)(2,1)S(1)}, u32[]{:S(2)}, u32[]{:S(2)}) collective-permute-start(bf16[256,1152]{1,0:T(8,128)(2,1)S(1)} %get-tuple-element.18.v), channel_id=1, source_target_pairs={{0,1},{1,0},{2,3},{3,2},{4,5},{5,4},{6,7},{7,6},{8,9},{9,8},{10,11... | collective-permute-start | bytes 1769480 | tf_op jit(solution)/shard_map/ppermute | solution.py:61
  52.8 14.4 %collective-permute-start.8 = (bf16[256,1152]{1,0:T(8,128)(2,1)S(1)}, bf16[256,1152]{1,0:T(8,128)(2,1)S(1)}, u32[]{:S(2)}, u32[]{:S(2)}) collective-permute-start(bf16[256,1152]{1,0:T(8,128)(2,1)S(1)} %collective-permute-done.7.across), channel_id=1, source_target_pairs={{0,1},{1,0},{2,3},{3,2},{4,5},{5,4},{6,7},{7,6},{8,9},{9,8},{10,11... | collective-permute-start | bytes 1769480 | tf_op jit(solution)/shard_map/ppermute | solution.py:61
  59.3 12.3 %copy-start.1 = (f32[256,1152]{1,0:T(8,128)S(1)}, f32[256,1152]{1,0:T(8,128)}, u32[]{:S(2)}) copy-start(f32[256,1152]{1,0:T(8,128)} %images.7) | copy-start | bytes 3538948
  59.3 12.4 %copy-start.3 = (f32[256,1152]{1,0:T(8,128)S(1)}, f32[256,1152]{1,0:T(8,128)}, u32[]{:S(2)}) copy-start(f32[256,1152]{1,0:T(8,128)} %texts.7) | copy-start | bytes 3538948
  59.3 15.2 %collective-permute-start.1 = (bf16[256,1152]{1,0:T(8,128)(2,1)S(1)}, bf16[256,1152]{1,0:T(8,128)(2,1)S(1)}, u32[]{:S(2)}, u32[]{:S(2)}) collective-permute-start(bf16[256,1152]{1,0:T(8,128)(2,1)S(1)} %collective-permute-done.near), channel_id=1, source_target_pairs={{0,1},{2,3},{3,2},{4,5},{5,4},{6,7},{7,6},{8,9},{9,8},{10,11},{11,... | collective-permute-start | bytes 1769480 | tf_op jit(solution)/shard_map/ppermute | solution.py:61
  60.8 13.8 %collective-permute-start.4 = (bf16[256,1152]{1,0:T(8,128)(2,1)S(1)}, bf16[256,1152]{1,0:T(8,128)(2,1)S(1)}, u32[]{:S(2)}, u32[]{:S(2)}) collective-permute-start(bf16[256,1152]{1,0:T(8,128)(2,1)S(1)} %collective-permute-done.near), channel_id=1, source_target_pairs={{2,1},{3,4},{4,3},{5,6},{6,5},{7,8},{8,7},{9,10},{10,9},{11,12},{1... | collective-permute-start | bytes 1769480 | tf_op jit(solution)/shard_map/ppermute | solution.py:61
  62.1 12.5 %collective-permute-start.3 = (bf16[256,1152]{1,0:T(8,128)(2,1)S(1)}, bf16[256,1152]{1,0:T(8,128)(2,1)S(1)}, u32[]{:S(2)}, u32[]{:S(2)}) collective-permute-start(bf16[256,1152]{1,0:T(8,128)(2,1)S(1)} %collective-permute-done.2.turned.leap), channel_id=1, source_target_pairs={{1,0},{14,15},{17,16},{30,31},{33,32},{46,47},{49,48},{62,63},{65,... | collective-permute-start | bytes 1769480 | tf_op jit(solution)/shard_map/ppermute | solution.py:61
  65.2 9.3 %collective-permute-start.5 = (bf16[256,1152]{1,0:T(8,128)(2,1)S(1)}, bf16[256,1152]{1,0:T(8,128)(2,1)S(1)}, u32[]{:S(2)}, u32[]{:S(2)}) collective-permute-start(bf16[256,1152]{1,0:T(8,128)(2,1)S(1)} %collective-permute-done.2.turned.leap), channel_id=1, source_target_pairs={{1,2},{14,13},{17,18},{30,29},{33,34},{46,45},{49,50},{62,61},{65,... | collective-permute-start | bytes 1769480 | tf_op jit(solution)/shard_map/ppermute | solution.py:61

commit v3 on v2

--- a/solution.py
+++ b/solution.py
@@ -31,30 +31,31 @@
 
 
 def routes():
-    near, across, turned, far, far_turned, swap, pass_near, pass_turned = [], [], [], [], [], [], [], []
+    names = ("near", "across", "turned", "far", "far_turned", "swap", "pass_near", "pass_turned")
+    pairs = {name: [] for name in names}
     for k in range(COUNT):
         x, y, z, core = place(k)
         edge = 7 if core == 1 else 0
         way = 1 if core == 1 else -1
         one, two, three = (k + way) % COUNT, (k + 2 * way) % COUNT, (k + 3 * way) % COUNT
-        swap.append((k, k ^ 1))
-        across.append((k, (k - 2 * way) % COUNT))
+        pairs["swap"].append((k, k ^ 1))
+        pairs["across"].append((k, (k - 2 * way) % COUNT))
         if y == edge:
-            stop = INDEX[(x, 7 - edge, z, core)]
-            near.append((k, stop))
-            turned.append((stop, two))
+            stop = INDEX[(place(two)[0], 7 - edge, z, core)]
+            pairs["near"].append((k, stop))
+            pairs["turned"].append((stop, two))
         else:
-            near.append((k, two))
+            pairs["near"].append((k, two))
             if y != 7 - edge:
-                far.append((k, one))
+                pairs["far"].append((k, one))
         if y == edge - way:
-            turned.append((k, three))
+            pairs["turned"].append((k, three))
         if y == 7 - edge:
-            pass_turned.append((k, k ^ 1))
-            far_turned.append((k, one))
+            pairs["pass_turned"].append((k, k ^ 1))
+            pairs["far_turned"].append((k, one))
         else:
-            pass_near.append((k, k ^ 1))
-    return near, across, turned, far, far_turned, swap, pass_near, pass_turned
+            pairs["pass_near"].append((k, k ^ 1))
+    return pairs
 
 
 def send(value, pairs):
@@ -97,7 +98,22 @@
         values = wide[rows]
         size = jnp.sqrt(jnp.sum(values * values, axis=-1, keepdims=True) + 1e-06)
         norm[rows] = size
-        half[rows] = (values / size).astype(HALF)
+        half[rows] = (values * (1.0 / size)).astype(HALF)
+
+
+def gate_kernel(*refs):
+    pass
+
+
+def after(value, *others):
+    return pl.pallas_call(
+        gate_kernel,
+        out_shape=jax.ShapeDtypeStruct(value.shape, value.dtype),
+        in_specs=[HBM] * (1 + len(others)),
+        out_specs=HBM,
+        input_output_aliases={0: 0},
+        compiler_params=PARAMS,
+    )(value, *others)
 
 
 def tile(consts, own, other, diagonal, loss, logits, dlogit):
@@ -111,45 +127,49 @@
             same = lax.broadcasted_iota(jnp.int32, shape, 0) + i * PIECE == lax.broadcasted_iota(jnp.int32, shape, 1)
             value = jnp.where(same, -value, value)
         small = jnp.exp(-jnp.abs(value))
-        loss[rows] += jnp.sum(jnp.maximum(value, 0.0) + jnp.log1p(small), axis=-1, keepdims=True)
-        grad = jnp.where(value >= 0, 1.0, small) / (1.0 + small) * scale
+        loss[rows] += jnp.sum(jnp.maximum(value, 0.0) + jnp.log(1.0 + small), axis=-1, keepdims=True)
+        grad = jnp.where(value >= 0, scale, scale * small) * pl.reciprocal(1.0 + small)
         if diagonal:
             grad = jnp.where(same, -grad, grad)
         dlogit[rows] = grad.astype(HALF)
 
 
-def add_grad(grad, dlogit, other, fresh=False):
+def add_grad(grad, dlogit, other, fresh=False, base=None):
     for i in range(grad.shape[1] // LANES):
         cols = pl.ds(i * LANES, LANES)
         part = jnp.dot(dlogit[...], other[:, cols], preferred_element_type=WIDE)
-        grad[:, cols] = part if fresh else grad[:, cols] + part
-
-
-def first_kernel(consts, u, v, beside, across, passed, grad_u, grad_v, loss_u, loss_v, logits, dlogit):
+        grad[:, cols] = part if fresh else (grad if base is None else base)[:, cols] + part
+
+
+def first_kernel(consts, u, v, grad_u, grad_v, loss_u, loss_v, logits, dlogit):
     loss_u[...] = jnp.zeros_like(loss_u)
     loss_v[...] = jnp.zeros_like(loss_v)
-    for own, grad, loss, others in ((u, grad_u, loss_u, (v, across)), (v, grad_v, loss_v, (u, beside, passed))):
+    for own, grad, loss, others in ((u, grad_u, loss_u, (v,)), (v, grad_v, loss_v, (u,))):
         for i, other in enumerate(others):
             tile(consts, own, other, i == 0, loss, logits, dlogit)
             add_grad(grad, dlogit, other, i == 0)
 
 
 def back(rows, values, norm, grad):
-    size = norm[rows]
-    unit = values / size
+    inverse = 1.0 / norm[rows]
     value = grad[rows]
-    along = jnp.sum(unit * value, axis=-1, keepdims=True)
-    return (value - unit * along) / size
-
-
-def second_kernel(consts, v, near, turned, images, texts, norm_v, grad_v_in, loss_v_in, grad_v, loss_v,
-                  logits, dlogit, block, wide, sems):
+    along = jnp.sum(values * value, axis=-1, keepdims=True) * (inverse * inverse)
+    return (value - values * along) * inverse
+
+
+def second_kernel(consts, u, v, beside, across, passed, near, turned, images, texts, norm_v, grad_u_in, grad_v_in, loss_u_in,
+                  loss_v_in, grad_u, grad_v, loss_u, loss_v, logits, dlogit, block, wide, sems):
     core, y = rows_place()
     fetch(core == 0, images, texts, wide, sems, True)
-    edge = jnp.where(core == 0, 7, 0)
+    loss_u[...] = loss_u_in[...]
     loss_v[...] = loss_v_in[...]
-    grad_v[...] = grad_v_in[...]
-    block[...] = jnp.where(y == edge, turned[...], near[...])
+    tile(consts, u, across, False, loss_u, logits, dlogit)
+    add_grad(grad_u, dlogit, across, base=grad_u_in)
+    tile(consts, v, beside, False, loss_v, logits, dlogit)
+    add_grad(grad_v, dlogit, beside, base=grad_v_in)
+    tile(consts, v, passed, False, loss_v, logits, dlogit)
+    add_grad(grad_v, dlogit, passed)
+    block[...] = jnp.where(y == jnp.where(core == 0, 7, 0), turned[...], near[...])
     tile(consts, v, block, False, loss_v, logits, dlogit)
     add_grad(grad_v, dlogit, block)
     for i in range(wide.shape[0] // PIECE):
@@ -174,10 +194,9 @@
 
     edge, after = jnp.where(core == 0, 0, 7), jnp.where(core == 0, 1, 6)
     loss_u[...] = loss_u_in[...]
-    grad_u[...] = grad_u_in[...]
     block[...] = jnp.where(y == edge, passed_turned[...], passed[...])
     tile(consts, u, block, False, loss_u, logits, dlogit)
-    add_grad(grad_u, dlogit, block)
+    add_grad(grad_u, dlogit, block, base=grad_u_in)
     block[...] = jnp.where(y == edge, leap[...], jnp.where(y == after, far_turned[...], far[...]))
     tile(consts, u, block, False, loss_u, logits, dlogit)
     add_grad(grad_u, dlogit, block)
@@ -203,16 +222,16 @@
 
 VMEM = pl.BlockSpec(memory_space=pltpu.VMEM)
 SMEM = pl.BlockSpec(memory_space=pltpu.SMEM)
-HBM = pl.BlockSpec(memory_space=pltpu.HBM)
+HBM = pl.BlockSpec(memory_space=pl.ANY)
 PARAMS = pltpu.CompilerParams(vmem_limit_bytes=24 * 2**20)
 
 
 def cost(tiles):
-    return pl.CostEstimate(flops=tiles * 40 * 256 * 256 * 1152, bytes_accessed=4 * 2**20, transcendentals=0)
+    return pl.CostEstimate(flops=int(tiles * 40) * 256 * 256 * 1152, bytes_accessed=4 * 2**20, transcendentals=0)
 
 
 def local(images, texts, log_temp, bias):
-    near_to, across_to, turned_to, far_to, far_turned_to, swap_to, pass_near_to, pass_turned_to = routes()
+    pairs = routes()
     count, width = images.shape
     pieces = count // PIECE
     consts = jnp.concatenate([log_temp, bias])
@@ -226,47 +245,47 @@
     column_room = pltpu.VMEM((count, 1), WIDE)
     sems = pltpu.SemaphoreType.DMA((pieces,))
 
-    def unit(swap):
+    def unit(swap, room):
         return pl.pallas_call(
             functools.partial(unit_kernel, swap),
             out_shape=(half, column),
             in_specs=[HBM, HBM],
             out_specs=(VMEM, VMEM),
             scratch_shapes=[wide_room, sems],
-            compiler_params=PARAMS,
+            compiler_params=pltpu.CompilerParams(vmem_limit_bytes=room * 2**20),
         )(images, texts)
 
     _, y = rows_place()
-    u, norm_u = unit(False)
-    near = send(u, near_to)
-    v, norm_v = unit(True)
-    across = send(v, across_to)
-    turned = send(jnp.where((y == 0) | (y == 7), near, u), turned_to)
-    beside = send(v, swap_to)
-    far = send(near, far_to)
-    passed_near = send(near, pass_near_to)
-    passed_across = send(across, swap_to)
-    far_turned = send(turned, far_turned_to)
-    passed_turned = send(turned, pass_turned_to)
-
+    u, norm_u = unit(False, 24)
+    near = send(u, pairs["near"])
+    v, norm_v = unit(True, 24)
+    across = send(v, pairs["across"])
+    turned = send(jnp.where((y == 0) | (y == 7), near, u), pairs["turned"])
+    beside = send(v, pairs["swap"])
+    far = send(near, pairs["far"])
+    passed_near = send(near, pairs["pass_near"])
+    passed_across = send(across, pairs["swap"])
     grad_u, grad_v, loss_u, loss_v = pl.pallas_call(
         first_kernel,
         out_shape=(wide, wide, column, column),
-        in_specs=[SMEM] + [VMEM] * 5,
+        in_specs=[SMEM] + [VMEM] * 2,
         out_specs=(VMEM,) * 4,
         scratch_shapes=[logits, dlogit],
         compiler_params=PARAMS,
-        cost_estimate=cost(5),
-    )(consts, u, v, beside, across, passed_across)
-    grad_v, loss_v = pl.pallas_call(
+        cost_estimate=cost(0.1),
+    )(consts, u, v)
+    turned = after(turned, loss_u, far, passed_near)
+    far_turned = send(turned, pairs["far_turned"])
+    passed_turned = send(turned, pairs["pass_turned"])
+    grad_u, grad_v, loss_u, loss_v = pl.pallas_call(
         second_kernel,
-        out_shape=(wide, column),
-        in_specs=[SMEM] + [VMEM] * 3 + [HBM] * 2 + [VMEM] * 3,
-        out_specs=(VMEM,) * 2,
+        out_shape=(wide, wide, column, column),
+        in_specs=[SMEM] + [VMEM] * 7 + [HBM] * 2 + [VMEM] * 5,
+        out_specs=(VMEM,) * 4,
         scratch_shapes=[logits, dlogit, half_room, wide_room, sems],
         compiler_params=PARAMS,
-        cost_estimate=cost(1),
-    )(consts, v, near, turned, images, texts, norm_v, grad_v, loss_v)
+        cost_estimate=cost(3),
+    )(consts, u, v, beside, across, passed_across, near, turned, images, texts, norm_v, grad_u, grad_v, loss_u, loss_v)
     row_loss, image_grad, text_grad = pl.pallas_call(
         last_kernel,
         out_shape=(jax.ShapeDtypeStruct((1, count), WIDE), wide, wide),

time: 80.6 us -> 77.8 us (0.965); the launches traced: 79.2 us -> 77.4 us
  waiting for transfers between devices: 21.8 us -> 18.8 us
  starting transfers between devices: 38.9 us -> 40.9 us
    ppermute x9, waiting for transfers between devices: 21.8 us -> 18.8 us  [send(): return lax.ppermute(value, AXES, pairs)]
    pallas_call x1, Pallas kernels: 4.53 us -> 2.06 us  [local(): pl.pallas_call(first_kernel, out_shape=(wide, wide, column, column), in_s...]
    ppermute x9, starting transfers between devices: 38.9 us -> 40.9 us  [send(): return lax.ppermute(value, AXES, pairs)]
    pallas_call x1 -> x2, Pallas kernels: 2.8 us -> 4.64 us  [the longest x1 4.63 us: local(): pl.pallas_call(second_kernel, out_shape=(wide, wide, column, column), in_...]
  transfers between devices with their start and end apart: 9 -> 9, of which waited for: 1 -> 2; matrix products, arithmetic and copies ran while one was open for 0% -> 0% of each run, Pallas kernels for 10% -> 10%
where the time goes in v3:
time: 77.8 us; the launch traced here: 77.4 us
  starting transfers between devices  40.9 us (53%)
  waiting for transfers between devices  18.8 us (24%)
  Pallas kernels  12.8 us (16%)
  local copies, waits for them, and re-layouts  2.55 us (3%)
  between operations  2.18 us (3%)
    ppermute x9, starting transfers between devices, send(): return lax.ppermute(value, AXES, pairs)  40.9 us
    ppermute x9, waiting for transfers between devices, send(): return lax.ppermute(value, AXES, pairs)  18.8 us
    pallas_call x1, Pallas kernels, local(): pl.pallas_call(second_kernel, out_shape=(wide, wide, column, column), in_...  4.63 us
    pallas_call x1, Pallas kernels, local(): pl.pallas_call(last_kernel, out_shape=(jax.ShapeDtypeStruct((1, count), W...  4.51 us
    unnamed x8, local copies, waits for them, and re-layouts  2.55 us
    pallas_call x1, Pallas kernels, local(): pl.pallas_call(first_kernel, out_shape=(wide, wide, column, column), in_s...  2.06 us
    pallas_call x2, Pallas kernels, unit(): pl.pallas_call(functools.partial(unit_kernel, swap), out_shape=(half, col...  1.63 us
  transfers between devices with their start and end apart: 9, of which 2 were waited for; matrix products, arithmetic and copies ran while one was open for 0% of the time, Pallas kernels for 10%

profile of v3, /device:TPU:1, one launch (start us, length us, event | category | flops | bytes accessed | tf_op | source)
XLA Modules:
  0.0 77.4 jit_solution(3142508018869730659)
XLA Ops:
  0.6 0.0 copy-start
  0.6 1.3 %copy-done = f32[256,1152]{1,0:T(8,128)S(1)} copy-done((f32[256,1152]{1,0:T(8,128)S(1)}, f32[256,1152]{1,0:T(8,128)}, u32[]{:S(2)}) %copy-start) | copy-done | bytes 1179672
  1.9 0.0 copy-start.2
  1.9 1.3 %copy-done.2 = f32[256,1152]{1,0:T(8,128)S(1)} copy-done((f32[256,1152]{1,0:T(8,128)S(1)}, f32[256,1152]{1,0:T(8,128)}, u32[]{:S(2)}) %copy-start.2) | copy-done | bytes 1179672
  3.2 0.8 %shard_map.67 = (bf16[256,1152]{1,0:T(8,128)(2,1)S(1)}, f32[256,1]{1,0:T(8,128)S(1)}) custom-call(f32[256,1152]{1,0:T(8,128)S(1)} %copy-done, f32[256,1152]{1,0:T(8,128)S(1)} %copy-done.2), custom_call_target="tpu_custom_call" | custom-call | tf_op jit(solution)/shard_map/pallas_call | solution.py:249
  4.0 4.0 %collective-permute-start = (bf16[256,1152]{1,0:T(8,128)(2,1)S(1)}, bf16[256,1152]{1,0:T(8,128)(2,1)S(1)}, u32[]{:S(2)}, u32[]{:S(2)}) collective-permute-start(bf16[256,1152]{1,0:T(8,128)(2,1)S(1)} %get-tuple-element.18.u), channel_id=1, source_target_pairs={{0,158},{1,3},{2,0},{3,5},{4,2},{5,7},{6,4},{7,9},{8,6},{9,11},{10... | collective-permute-start | bytes 1769480 | tf_op jit(solution)/shard_map/ppermute | solution.py:62
  8.0 0.8 %shard_map.68 = (bf16[256,1152]{1,0:T(8,128)(2,1)S(1)}, f32[256,1]{1,0:T(8,128)S(1)}) custom-call(f32[256,1152]{1,0:T(8,128)S(1)} %copy-done, f32[256,1152]{1,0:T(8,128)S(1)} %copy-done.2), custom_call_target="tpu_custom_call" | custom-call | tf_op jit(solution)/shard_map/pallas_call | solution.py:249
  8.9 18.1 %collective-permute-start.7 = (bf16[256,1152]{1,0:T(8,128)(2,1)S(1)}, bf16[256,1152]{1,0:T(8,128)(2,1)S(1)}, u32[]{:S(2)}, u32[]{:S(2)}) collective-permute-start(bf16[256,1152]{1,0:T(8,128)(2,1)S(1)} %get-tuple-element.19.v), channel_id=1, source_target_pairs={{0,2},{1,767},{2,4},{3,1},{4,6},{5,3},{6,8},{7,5},{8,10},{9,7},{10... | collective-permute-start | bytes 1769480 | tf_op jit(solution)/shard_map/ppermute | solution.py:62
  27.0 0.0 collective-permute-done.near
  27.1 0.1 broadcast_select_fusion
  27.1 1.9 %collective-permute-start.2 = (bf16[256,1152]{1,0:T(8,128)(2,1)S(1)}, bf16[256,1152]{1,0:T(8,128)(2,1)S(1)}, u32[]{:S(2)}, u32[]{:S(2)}) collective-permute-start(bf16[256,1152]{1,0:T(8,128)(2,1)S(1)} %broadcast_select_fusion), channel_id=1, source_target_pairs={{158,766},{2,767},{13,16},{1,17},{30,14},{18,15},{29,32},{17,33},{... | collective-permute-start | bytes 1769480 | tf_op jit(solution)/shard_map/ppermute | solution.py:62
  29.1 1.3 %collective-permute-start.3 = (bf16[256,1152]{1,0:T(8,128)(2,1)S(1)}, bf16[256,1152]{1,0:T(8,128)(2,1)S(1)}, u32[]{:S(2)}, u32[]{:S(2)}) collective-permute-start(bf16[256,1152]{1,0:T(8,128)(2,1)S(1)} %collective-permute-done.near), channel_id=1, source_target_pairs={{2,1},{3,4},{4,3},{5,6},{6,5},{7,8},{8,7},{9,10},{10,9},{11,12},{1... | collective-permute-start | bytes 1769480 | tf_op jit(solution)/shard_map/ppermute | solution.py:62
  30.4 1.3 %collective-permute-start.1 = (bf16[256,1152]{1,0:T(8,128)(2,1)S(1)}, bf16[256,1152]{1,0:T(8,128)(2,1)S(1)}, u32[]{:S(2)}, u32[]{:S(2)}) collective-permute-start(bf16[256,1152]{1,0:T(8,128)(2,1)S(1)} %collective-permute-done.near), channel_id=1, source_target_pairs={{0,1},{2,3},{3,2},{4,5},{5,4},{6,7},{7,6},{8,9},{9,8},{10,11},{11,... | collective-permute-start | bytes 1769480 | tf_op jit(solution)/shard_map/ppermute | solution.py:62
  31.7 3.1 %collective-permute-start.6 = (bf16[256,1152]{1,0:T(8,128)(2,1)S(1)}, bf16[256,1152]{1,0:T(8,128)(2,1)S(1)}, u32[]{:S(2)}, u32[]{:S(2)}) collective-permute-start(bf16[256,1152]{1,0:T(8,128)(2,1)S(1)} %get-tuple-element.19.v), channel_id=1, source_target_pairs={{0,1},{1,0},{2,3},{3,2},{4,5},{5,4},{6,7},{7,6},{8,9},{9,8},{10,11... | collective-permute-start | bytes 1769480 | tf_op jit(solution)/shard_map/ppermute | solution.py:62
  34.7 18.0 %collective-permute-done.7.across = bf16[256,1152]{1,0:T(8,128)(2,1)S(1)} collective-permute-done((bf16[256,1152]{1,0:T(8,128)(2,1)S(1)}, bf16[256,1152]{1,0:T(8,128)(2,1)S(1)}, u32[]{:S(2)}, u32[]{:S(2)}) %collective-permute-start.7) | collective-permute-done | bytes 589856 | tf_op jit(solution)/shard_map/ppermute | solution.py:62
  52.8 5.3 %collective-permute-start.8 = (bf16[256,1152]{1,0:T(8,128)(2,1)S(1)}, bf16[256,1152]{1,0:T(8,128)(2,1)S(1)}, u32[]{:S(2)}, u32[]{:S(2)}) collective-permute-start(bf16[256,1152]{1,0:T(8,128)(2,1)S(1)} %collective-permute-done.7.across), channel_id=1, source_target_pairs={{0,1},{1,0},{2,3},{3,2},{4,5},{5,4},{6,7},{7,6},{8,9},{9,8},{10,11... | collective-permute-start | bytes 1769480 | tf_op jit(solution)/shard_map/ppermute | solution.py:62
  59.3 0.1 pad_maximum_fusion.consts
  59.4 2.1 %shard_map.69 = (f32[256,1152]{1,0:T(8,128)S(1)}, f32[256,1152]{1,0:T(8,128)S(1)}, f32[256,1]{1,0:T(8,128)S(1)}, f32[256,1]{1,0:T(8,128)S(1)}) custom-call(f32[2]{0:T(128)S(1)} %pad_maximum_fusion.consts, bf16[256,1152]{1,0:T(8,128)(2,1)S(1)} %get-tuple-element.18.u, bf16[256,1152]{1,0:T(8,128)(2,1)S(1)} %get-tuple-element.19.v), custom_call_target="tpu_custom_call" | custom-call | flops 301989888 | bytes 4194304 | tf_op jit(solution)/shard_map/pallas_call | solution.py:268
  61.4 0.0 collective-permute-done.2.refs_0_
  61.5 0.0 collective-permute-done.3.refs_2_.far
  61.5 0.0 collective-permute-done.1.refs_3_.passed
  61.5 0.0 copy-start.1
  61.5 0.0 copy-start.3
  61.5 4.6 %collective-permute-start.5 = (bf16[256,1152]{1,0:T(8,128)(2,1)S(1)}, bf16[256,1152]{1,0:T(8,128)(2,1)S(1)}, u32[]{:S(2)}, u32[]{:S(2)}) collective-permute-start(bf16[256,1152]{1,0:T(8,128)(2,1)S(1)} %shard_map.70.turned.leap), channel_id=1, source_target_pairs={{1,2},{14,13},{17,18},{30,29},{33,34},{46,45},{49,50},{62,61},{65,... | collective-permute-start | bytes 1769480 | tf_op jit(solution)/shard_map/ppermute | solution.py:62
  66.1 1.3 %collective-permute-start.4 = (bf16[256,1152]{1,0:T(8,128)(2,1)S(1)}, bf16[256,1152]{1,0:T(8,128)(2,1)S(1)}, u32[]{:S(2)}, u32[]{:S(2)}) collective-permute-start(bf16[256,1152]{1,0:T(8,128)(2,1)S(1)} %shard_map.70.turned.leap), channel_id=1, source_target_pairs={{1,0},{14,15},{17,16},{30,31},{33,32},{46,47},{49,48},{62,63},{65,... | collective-permute-start | bytes 1769480 | tf_op jit(solution)/shard_map/ppermute | solution.py:62
  67.5 0.0 collective-permute-done.6.beside
  67.5 0.0 collective-permute-done.8.passed
  67.5 0.0 copy-done.1
  67.5 0.0 copy-done.3
  67.5 4.6 %shard_map.71 = (f32[256,1152]{1,0:T(8,128)S(1)}, f32[256,1152]{1,0:T(8,128)S(1)}, f32[256,1]{1,0:T(8,128)S(1)}, f32[256,1]{1,0:T(8,128)S(1)}) custom-call(f32[2]{0:T(128)S(1)} %pad_maximum_fusion.consts, bf16[256,1152]{1,0:T(8,128)(2,1)S(1)} %get-tuple-element.18.u, bf16[256,1152]{1,0:T(8,128)(2,1)S(1)} %get-tuple-element.19.v, ...), custom_call_target="tpu_custom_call" | custom-call | flops 9059696640 | bytes 4194304 | tf_op jit(solution)/shard_map/pallas_call | solution.py:280
  72.2 0.8 collective-permute-done.5.far_turned
  72.9 0.0 collective-permute-done.4.passed_turned
  72.9 4.5 %shard_map.72 = (f32[1,256]{1,0:T(1,128)}, f32[256,1152]{1,0:T(8,128)}, f32[256,1152]{1,0:T(8,128)}) custom-call(f32[2]{0:T(128)S(1)} %pad_maximum_fusion.consts, bf16[256,1152]{1,0:T(8,128)(2,1)S(1)} %get-tuple-element.18.u, bf16[256,1152]{1,0:T(8,128)(2,1)S(1)} %collective-permute-done.1.refs_3_.passed, ...), custom_call_target="tpu_custom_call" | custom-call | flops 6039797760 | bytes 4194304 | tf_op jit(solution)/shard_map/pallas_call | solution.py:289
  (1 shorter events, 0.0 us)
Async XLA Ops:
  0.6 1.3 %copy-start = (f32[256,1152]{1,0:T(8,128)S(1)}, f32[256,1152]{1,0:T(8,128)}, u32[]{:S(2)}) copy-start(f32[256,1152]{1,0:T(8,128)} %images.7) | copy-start | bytes 3538948
  1.9 1.3 %copy-start.2 = (f32[256,1152]{1,0:T(8,128)S(1)}, f32[256,1152]{1,0:T(8,128)}, u32[]{:S(2)}) copy-start(f32[256,1152]{1,0:T(8,128)} %texts.7) | copy-start | bytes 3538948
  4.0 23.1 %collective-permute-start = (bf16[256,1152]{1,0:T(8,128)(2,1)S(1)}, bf16[256,1152]{1,0:T(8,128)(2,1)S(1)}, u32[]{:S(2)}, u32[]{:S(2)}) collective-permute-start(bf16[256,1152]{1,0:T(8,128)(2,1)S(1)} %get-tuple-element.18.u), channel_id=1, source_target_pairs={{0,158},{1,3},{2,0},{3,5},{4,2},{5,7},{6,4},{7,9},{8,6},{9,11},{10... | collective-permute-start | bytes 1769480 | tf_op jit(solution)/shard_map/ppermute | solution.py:62
  8.9 43.9 %collective-permute-start.7 = (bf16[256,1152]{1,0:T(8,128)(2,1)S(1)}, bf16[256,1152]{1,0:T(8,128)(2,1)S(1)}, u32[]{:S(2)}, u32[]{:S(2)}) collective-permute-start(bf16[256,1152]{1,0:T(8,128)(2,1)S(1)} %get-tuple-element.19.v), channel_id=1, source_target_pairs={{0,2},{1,767},{2,4},{3,1},{4,6},{5,3},{6,8},{7,5},{8,10},{9,7},{10... | collective-permute-start | bytes 1769480 | tf_op jit(solution)/shard_map/ppermute | solution.py:62
  27.1 34.3 %collective-permute-start.2 = (bf16[256,1152]{1,0:T(8,128)(2,1)S(1)}, bf16[256,1152]{1,0:T(8,128)(2,1)S(1)}, u32[]{:S(2)}, u32[]{:S(2)}) collective-permute-start(bf16[256,1152]{1,0:T(8,128)(2,1)S(1)} %broadcast_select_fusion), channel_id=1, source_target_pairs={{158,766},{2,767},{13,16},{1,17},{30,14},{18,15},{29,32},{17,33},{... | collective-permute-start | bytes 1769480 | tf_op jit(solution)/shard_map/ppermute | solution.py:62
  29.1 32.4 %collective-permute-start.3 = (bf16[256,1152]{1,0:T(8,128)(2,1)S(1)}, bf16[256,1152]{1,0:T(8,128)(2,1)S(1)}, u32[]{:S(2)}, u32[]{:S(2)}) collective-permute-start(bf16[256,1152]{1,0:T(8,128)(2,1)S(1)} %collective-permute-done.near), channel_id=1, source_target_pairs={{2,1},{3,4},{4,3},{5,6},{6,5},{7,8},{8,7},{9,10},{10,9},{11,12},{1... | collective-permute-start | bytes 1769480 | tf_op jit(solution)/shard_map/ppermute | solution.py:62
  30.4 31.1 %collective-permute-start.1 = (bf16[256,1152]{1,0:T(8,128)(2,1)S(1)}, bf16[256,1152]{1,0:T(8,128)(2,1)S(1)}, u32[]{:S(2)}, u32[]{:S(2)}) collective-permute-start(bf16[256,1152]{1,0:T(8,128)(2,1)S(1)} %collective-permute-done.near), channel_id=1, source_target_pairs={{0,1},{2,3},{3,2},{4,5},{5,4},{6,7},{7,6},{8,9},{9,8},{10,11},{11,... | collective-permute-start | bytes 1769480 | tf_op jit(solution)/shard_map/ppermute | solution.py:62
  31.7 35.8 %collective-permute-start.6 = (bf16[256,1152]{1,0:T(8,128)(2,1)S(1)}, bf16[256,1152]{1,0:T(8,128)(2,1)S(1)}, u32[]{:S(2)}, u32[]{:S(2)}) collective-permute-start(bf16[256,1152]{1,0:T(8,128)(2,1)S(1)} %get-tuple-element.19.v), channel_id=1, source_target_pairs={{0,1},{1,0},{2,3},{3,2},{4,5},{5,4},{6,7},{7,6},{8,9},{9,8},{10,11... | collective-permute-start | bytes 1769480 | tf_op jit(solution)/shard_map/ppermute | solution.py:62
  52.8 14.7 %collective-permute-start.8 = (bf16[256,1152]{1,0:T(8,128)(2,1)S(1)}, bf16[256,1152]{1,0:T(8,128)(2,1)S(1)}, u32[]{:S(2)}, u32[]{:S(2)}) collective-permute-start(bf16[256,1152]{1,0:T(8,128)(2,1)S(1)} %collective-permute-done.7.across), channel_id=1, source_target_pairs={{0,1},{1,0},{2,3},{3,2},{4,5},{5,4},{6,7},{7,6},{8,9},{9,8},{10,11... | collective-permute-start | bytes 1769480 | tf_op jit(solution)/shard_map/ppermute | solution.py:62
  61.5 6.0 %copy-start.1 = (f32[256,1152]{1,0:T(8,128)S(1)}, f32[256,1152]{1,0:T(8,128)}, u32[]{:S(2)}) copy-start(f32[256,1152]{1,0:T(8,128)} %images.7) | copy-start | bytes 3538948
  61.5 6.0 %copy-start.3 = (f32[256,1152]{1,0:T(8,128)S(1)}, f32[256,1152]{1,0:T(8,128)}, u32[]{:S(2)}) copy-start(f32[256,1152]{1,0:T(8,128)} %texts.7) | copy-start | bytes 3538948
  61.5 11.4 %collective-permute-start.5 = (bf16[256,1152]{1,0:T(8,128)(2,1)S(1)}, bf16[256,1152]{1,0:T(8,128)(2,1)S(1)}, u32[]{:S(2)}, u32[]{:S(2)}) collective-permute-start(bf16[256,1152]{1,0:T(8,128)(2,1)S(1)} %shard_map.70.turned.leap), channel_id=1, source_target_pairs={{1,2},{14,13},{17,18},{30,29},{33,34},{46,45},{49,50},{62,61},{65,... | collective-permute-start | bytes 1769480 | tf_op jit(solution)/shard_map/ppermute | solution.py:62
  66.1 6.8 %collective-permute-start.4 = (bf16[256,1152]{1,0:T(8,128)(2,1)S(1)}, bf16[256,1152]{1,0:T(8,128)(2,1)S(1)}, u32[]{:S(2)}, u32[]{:S(2)}) collective-permute-start(bf16[256,1152]{1,0:T(8,128)(2,1)S(1)} %shard_map.70.turned.leap), channel_id=1, source_target_pairs={{1,0},{14,15},{17,16},{30,31},{33,32},{46,47},{49,48},{62,63},{65,... | collective-permute-start | bytes 1769480 | tf_op jit(solution)/shard_map/ppermute | solution.py:62

commit v4 on v3

--- a/solution.py
+++ b/solution.py
@@ -31,7 +31,7 @@
 
 
 def routes():
-    names = ("near", "across", "turned", "far", "far_turned", "swap", "pass_near", "pass_turned")
+    names = ("near", "across", "leap", "turned", "far", "far_turned", "swap", "pass_near", "pass_turned")
     pairs = {name: [] for name in names}
     for k in range(COUNT):
         x, y, z, core = place(k)
@@ -49,7 +49,7 @@
             if y != 7 - edge:
                 pairs["far"].append((k, one))
         if y == edge - way:
-            pairs["turned"].append((k, three))
+            pairs["leap"].append((k, three))
         if y == 7 - edge:
             pairs["pass_turned"].append((k, k ^ 1))
             pairs["far_turned"].append((k, one))
@@ -105,7 +105,7 @@
     pass
 
 
-def after(value, *others):
+def after(value, *others, flops=0):
     return pl.pallas_call(
         gate_kernel,
         out_shape=jax.ShapeDtypeStruct(value.shape, value.dtype),
@@ -113,6 +113,7 @@
         out_specs=HBM,
         input_output_aliases={0: 0},
         compiler_params=PARAMS,
+        cost_estimate=pl.CostEstimate(flops=flops, bytes_accessed=0, transcendentals=0),
     )(value, *others)
 
 
@@ -255,16 +256,15 @@
             compiler_params=pltpu.CompilerParams(vmem_limit_bytes=room * 2**20),
         )(images, texts)
 
-    _, y = rows_place()
     u, norm_u = unit(False, 24)
     near = send(u, pairs["near"])
     v, norm_v = unit(True, 24)
     across = send(v, pairs["across"])
-    turned = send(jnp.where((y == 0) | (y == 7), near, u), pairs["turned"])
-    beside = send(v, pairs["swap"])
+    turned = send(near, pairs["turned"])
+    leap = send(u, pairs["leap"])
+    beside = send(after(v, near), pairs["swap"])
     far = send(near, pairs["far"])
     passed_near = send(near, pairs["pass_near"])
-    passed_across = send(across, pairs["swap"])
     grad_u, grad_v, loss_u, loss_v = pl.pallas_call(
         first_kernel,
         out_shape=(wide, wide, column, column),
@@ -274,7 +274,10 @@
         compiler_params=PARAMS,
         cost_estimate=cost(0.1),
     )(consts, u, v)
-    turned = after(turned, loss_u, far, passed_near)
+    across = after(across, leap, loss_u)
+    passed_across = send(across, pairs["swap"])
+    turned = after(turned, flops=35 * 10**8)
+    turned = after(turned, far, passed_near, beside)
     far_turned = send(turned, pairs["far_turned"])
     passed_turned = send(turned, pairs["pass_turned"])
     grad_u, grad_v, loss_u, loss_v = pl.pallas_call(
@@ -294,7 +297,7 @@
         scratch_shapes=[wide_room, column_room, logits, dlogit, half_room, wide_room, sems, sems, pltpu.SemaphoreType.DMA],
         compiler_params=PARAMS,
         cost_estimate=cost(2),
-    )(consts, u, passed_near, passed_turned, far, turned, far_turned, images, texts, norm_u, grad_u, grad_v, loss_u, loss_v)
+    )(consts, u, passed_near, passed_turned, far, leap, far_turned, images, texts, norm_u, grad_u, grad_v, loss_u, loss_v)
     return (row_loss.reshape(count), image_grad, text_grad)
 
 

time: 77.8 us -> 77.1 us (level)
  starting transfers between devices: 40.9 us -> 38.6 us
  waiting for transfers between devices: 18.8 us -> 20.5 us
    ppermute x9 -> x10, starting transfers between devices: 40.9 us -> 38.6 us  [send(): return lax.ppermute(value, AXES, pairs)]
    ppermute x9 -> x10, waiting for transfers between devices: 18.8 us -> 20.5 us  [send(): return lax.ppermute(value, AXES, pairs)]
    unnamed x8 -> x9, local copies, waits for them, and re-layouts: 2.55 us -> 2.59 us
  transfers between devices with their start and end apart: 9 -> 10, of which waited for: 2 -> 4; matrix products, arithmetic and copies ran while one was open for 0% -> 0% of each run, Pallas kernels for 10% -> 10%
where the time goes in v4:
time: 77.1 us; the launch traced here: 76.7 us
  starting transfers between devices  38.6 us (50%)
  waiting for transfers between devices  20.5 us (27%)
  Pallas kernels  12.9 us (17%)
  local copies, waits for them, and re-layouts  2.59 us (3%)
  between operations  2.12 us (3%)
    ppermute x10, starting transfers between devices, send(): return lax.ppermute(value, AXES, pairs)  38.6 us
    ppermute x10, waiting for transfers between devices, send(): return lax.ppermute(value, AXES, pairs)  20.5 us
    pallas_call x1, Pallas kernels, local(): pl.pallas_call(second_kernel, out_shape=(wide, wide, column, column), in_...  4.65 us
    pallas_call x1, Pallas kernels, local(): pl.pallas_call(last_kernel, out_shape=(jax.ShapeDtypeStruct((1, count), W...  4.52 us
    unnamed x9, local copies, waits for them, and re-layouts  2.59 us
    pallas_call x1, Pallas kernels, local(): pl.pallas_call(first_kernel, out_shape=(wide, wide, column, column), in_s...  2.06 us
    pallas_call x2, Pallas kernels, unit(): pl.pallas_call(functools.partial(unit_kernel, swap), out_shape=(half, col...  1.63 us
  transfers between devices with their start and end apart: 10, of which 4 were waited for; matrix products, arithmetic and copies ran while one was open for 0% of the time, Pallas kernels for 10%

profile of v4, /device:TPU:1, one launch (start us, length us, event | category | flops | bytes accessed | tf_op | source)
XLA Modules:
  0.0 76.7 jit_solution(3204196552310641199)
XLA Ops:
  0.6 0.0 copy-start
  0.6 1.3 %copy-done = f32[256,1152]{1,0:T(8,128)S(1)} copy-done((f32[256,1152]{1,0:T(8,128)S(1)}, f32[256,1152]{1,0:T(8,128)}, u32[]{:S(2)}) %copy-start) | copy-done | bytes 1179672
  1.9 0.0 copy-start.2
  1.9 1.3 %copy-done.2 = f32[256,1152]{1,0:T(8,128)S(1)} copy-done((f32[256,1152]{1,0:T(8,128)S(1)}, f32[256,1152]{1,0:T(8,128)}, u32[]{:S(2)}) %copy-start.2) | copy-done | bytes 1179672
  3.2 0.8 %shard_map.67 = (bf16[256,1152]{1,0:T(8,128)(2,1)S(1)}, f32[256,1]{1,0:T(8,128)S(1)}) custom-call(f32[256,1152]{1,0:T(8,128)S(1)} %copy-done, f32[256,1152]{1,0:T(8,128)S(1)} %copy-done.2), custom_call_target="tpu_custom_call" | custom-call | tf_op jit(solution)/shard_map/pallas_call | solution.py:250
  4.0 4.0 %collective-permute-start = (bf16[256,1152]{1,0:T(8,128)(2,1)S(1)}, bf16[256,1152]{1,0:T(8,128)(2,1)S(1)}, u32[]{:S(2)}, u32[]{:S(2)}) collective-permute-start(bf16[256,1152]{1,0:T(8,128)(2,1)S(1)} %get-tuple-element.18.u), channel_id=1, source_target_pairs={{0,158},{1,3},{2,0},{3,5},{4,2},{5,7},{6,4},{7,9},{8,6},{9,11},{10... | collective-permute-start | bytes 1769480 | tf_op jit(solution)/shard_map/ppermute | solution.py:62
  8.0 0.7 collective-permute-start.6
  8.7 0.8 %shard_map.69 = (bf16[256,1152]{1,0:T(8,128)(2,1)S(1)}, f32[256,1]{1,0:T(8,128)S(1)}) custom-call(f32[256,1152]{1,0:T(8,128)S(1)} %copy-done, f32[256,1152]{1,0:T(8,128)S(1)} %copy-done.2), custom_call_target="tpu_custom_call" | custom-call | tf_op jit(solution)/shard_map/pallas_call | solution.py:250
  9.6 18.7 %collective-permute-start.8 = (bf16[256,1152]{1,0:T(8,128)(2,1)S(1)}, bf16[256,1152]{1,0:T(8,128)(2,1)S(1)}, u32[]{:S(2)}, u32[]{:S(2)}) collective-permute-start(bf16[256,1152]{1,0:T(8,128)(2,1)S(1)} %get-tuple-element.19.v), channel_id=1, source_target_pairs={{0,2},{1,767},{2,4},{3,1},{4,6},{5,3},{6,8},{7,5},{8,10},{9,7},{10... | collective-permute-start | bytes 1769480 | tf_op jit(solution)/shard_map/ppermute | solution.py:62
  28.3 0.0 collective-permute-done.refs_1_.near
  28.3 1.9 %collective-permute-start.2 = (bf16[256,1152]{1,0:T(8,128)(2,1)S(1)}, bf16[256,1152]{1,0:T(8,128)(2,1)S(1)}, u32[]{:S(2)}, u32[]{:S(2)}) collective-permute-start(bf16[256,1152]{1,0:T(8,128)(2,1)S(1)} %collective-permute-done.refs_1_.near), channel_id=1, source_target_pairs={{158,766},{1,17},{30,14},{17,33},{46,30},{81,49},{14,46},{49,65},{... | collective-permute-start | bytes 1769480 | tf_op jit(solution)/shard_map/ppermute | solution.py:62
  31.6 0.1 pad_maximum_fusion.consts
  31.7 2.1 %shard_map.72 = (f32[256,1152]{1,0:T(8,128)S(1)}, f32[256,1152]{1,0:T(8,128)S(1)}, f32[256,1]{1,0:T(8,128)S(1)}, f32[256,1]{1,0:T(8,128)S(1)}) custom-call(f32[2]{0:T(128)S(1)} %pad_maximum_fusion.consts, bf16[256,1152]{1,0:T(8,128)(2,1)S(1)} %get-tuple-element.18.u, bf16[256,1152]{1,0:T(8,128)(2,1)S(1)} %get-tuple-element.19.v), custom_call_target="tpu_custom_call" | custom-call | flops 301989888 | bytes 4194304 | tf_op jit(solution)/shard_map/pallas_call | solution.py:268
  33.7 3.4 %collective-permute-start.4 = (bf16[256,1152]{1,0:T(8,128)(2,1)S(1)}, bf16[256,1152]{1,0:T(8,128)(2,1)S(1)}, u32[]{:S(2)}, u32[]{:S(2)}) collective-permute-start(bf16[256,1152]{1,0:T(8,128)(2,1)S(1)} %shard_map.70), channel_id=1, source_target_pairs={{0,1},{1,0},{2,3},{3,2},{4,5},{5,4},{6,7},{7,6},{8,9},{9,8},{10,11... | collective-permute-start | bytes 1769480 | tf_op jit(solution)/shard_map/ppermute | solution.py:62
  37.1 1.3 %collective-permute-start.1 = (bf16[256,1152]{1,0:T(8,128)(2,1)S(1)}, bf16[256,1152]{1,0:T(8,128)(2,1)S(1)}, u32[]{:S(2)}, u32[]{:S(2)}) collective-permute-start(bf16[256,1152]{1,0:T(8,128)(2,1)S(1)} %collective-permute-done.refs_1_.near), channel_id=1, source_target_pairs={{0,1},{2,3},{3,2},{4,5},{5,4},{6,7},{7,6},{8,9},{9,8},{10,11},{11,... | collective-permute-start | bytes 1769480 | tf_op jit(solution)/shard_map/ppermute | solution.py:62
  38.4 0.0 collective-permute-done.6.refs_1_.leap
  38.4 1.3 %collective-permute-start.3 = (bf16[256,1152]{1,0:T(8,128)(2,1)S(1)}, bf16[256,1152]{1,0:T(8,128)(2,1)S(1)}, u32[]{:S(2)}, u32[]{:S(2)}) collective-permute-start(bf16[256,1152]{1,0:T(8,128)(2,1)S(1)} %collective-permute-done.refs_1_.near), channel_id=1, source_target_pairs={{2,1},{3,4},{4,3},{5,6},{6,5},{7,8},{8,7},{9,10},{10,9},{11,12},{1... | collective-permute-start | bytes 1769480 | tf_op jit(solution)/shard_map/ppermute | solution.py:62
  39.7 14.3 %collective-permute-done.8.refs_0_ = bf16[256,1152]{1,0:T(8,128)(2,1)S(1)} collective-permute-done((bf16[256,1152]{1,0:T(8,128)(2,1)S(1)}, bf16[256,1152]{1,0:T(8,128)(2,1)S(1)}, u32[]{:S(2)}, u32[]{:S(2)}) %collective-permute-start.8) | collective-permute-done | bytes 589856 | tf_op jit(solution)/shard_map/ppermute | solution.py:62
  54.1 4.6 %collective-permute-start.9 = (bf16[256,1152]{1,0:T(8,128)(2,1)S(1)}, bf16[256,1152]{1,0:T(8,128)(2,1)S(1)}, u32[]{:S(2)}, u32[]{:S(2)}) collective-permute-start(bf16[256,1152]{1,0:T(8,128)(2,1)S(1)} %shard_map.73.across), channel_id=1, source_target_pairs={{0,1},{1,0},{2,3},{3,2},{4,5},{5,4},{6,7},{7,6},{8,9},{9,8},{10,11... | collective-permute-start | bytes 1769480 | tf_op jit(solution)/shard_map/ppermute | solution.py:62
  58.7 1.2 %collective-permute-done.2.refs_0_ = bf16[256,1152]{1,0:T(8,128)(2,1)S(1)} collective-permute-done((bf16[256,1152]{1,0:T(8,128)(2,1)S(1)}, bf16[256,1152]{1,0:T(8,128)(2,1)S(1)}, u32[]{:S(2)}, u32[]{:S(2)}) %collective-permute-start.2) | collective-permute-done | bytes 589856 | tf_op jit(solution)/shard_map/ppermute | solution.py:62
  59.9 0.0 copy-start.1
  59.9 0.0 copy-start.3
  59.9 0.0 collective-permute-done.4.refs_3_.beside
  59.9 0.0 collective-permute-done.1.refs_2_.passed
  59.9 2.9 %collective-permute-done.3.refs_1_.far = bf16[256,1152]{1,0:T(8,128)(2,1)S(1)} collective-permute-done((bf16[256,1152]{1,0:T(8,128)(2,1)S(1)}, bf16[256,1152]{1,0:T(8,128)(2,1)S(1)}, u32[]{:S(2)}, u32[]{:S(2)}) %collective-permute-start.3) | collective-permute-done | bytes 589856 | tf_op jit(solution)/shard_map/ppermute | solution.py:62
  62.8 1.3 %collective-permute-start.5 = (bf16[256,1152]{1,0:T(8,128)(2,1)S(1)}, bf16[256,1152]{1,0:T(8,128)(2,1)S(1)}, u32[]{:S(2)}, u32[]{:S(2)}) collective-permute-start(bf16[256,1152]{1,0:T(8,128)(2,1)S(1)} %shard_map.71.turned), channel_id=1, source_target_pairs={{1,0},{14,15},{17,16},{30,31},{33,32},{46,47},{49,48},{62,63},{65,... | collective-permute-start | bytes 1769480 | tf_op jit(solution)/shard_map/ppermute | solution.py:62
  64.1 1.3 %collective-permute-start.7 = (bf16[256,1152]{1,0:T(8,128)(2,1)S(1)}, bf16[256,1152]{1,0:T(8,128)(2,1)S(1)}, u32[]{:S(2)}, u32[]{:S(2)}) collective-permute-start(bf16[256,1152]{1,0:T(8,128)(2,1)S(1)} %shard_map.71.turned), channel_id=1, source_target_pairs={{1,2},{14,13},{17,18},{30,29},{33,34},{46,45},{49,50},{62,61},{65,... | collective-permute-start | bytes 1769480 | tf_op jit(solution)/shard_map/ppermute | solution.py:62
  65.4 0.0 collective-permute-done.9.passed
  65.5 0.0 copy-done.1
  65.5 0.0 copy-done.3
  65.5 4.6 %shard_map.74 = (f32[256,1152]{1,0:T(8,128)S(1)}, f32[256,1152]{1,0:T(8,128)S(1)}, f32[256,1]{1,0:T(8,128)S(1)}, f32[256,1]{1,0:T(8,128)S(1)}) custom-call(f32[2]{0:T(128)S(1)} %pad_maximum_fusion.consts, bf16[256,1152]{1,0:T(8,128)(2,1)S(1)} %get-tuple-element.18.u, bf16[256,1152]{1,0:T(8,128)(2,1)S(1)} %get-tuple-element.19.v, ...), custom_call_target="tpu_custom_call" | custom-call | flops 9059696640 | bytes 4194304 | tf_op jit(solution)/shard_map/pallas_call | solution.py:283
  70.1 0.0 collective-permute-done.5.passed_turned
  70.1 2.1 %collective-permute-done.7.far_turned = bf16[256,1152]{1,0:T(8,128)(2,1)S(1)} collective-permute-done((bf16[256,1152]{1,0:T(8,128)(2,1)S(1)}, bf16[256,1152]{1,0:T(8,128)(2,1)S(1)}, u32[]{:S(2)}, u32[]{:S(2)}) %collective-permute-start.7) | collective-permute-done | bytes 589856 | tf_op jit(solution)/shard_map/ppermute | solution.py:62
  72.2 4.5 %shard_map.75 = (f32[1,256]{1,0:T(1,128)}, f32[256,1152]{1,0:T(8,128)}, f32[256,1152]{1,0:T(8,128)}) custom-call(f32[2]{0:T(128)S(1)} %pad_maximum_fusion.consts, bf16[256,1152]{1,0:T(8,128)(2,1)S(1)} %get-tuple-element.18.u, bf16[256,1152]{1,0:T(8,128)(2,1)S(1)} %collective-permute-done.1.refs_2_.passed, ...), custom_call_target="tpu_custom_call" | custom-call | flops 6039797760 | bytes 4194304 | tf_op jit(solution)/shard_map/pallas_call | solution.py:292
  (5 shorter events, 0.1 us)
Async XLA Ops:
  0.6 1.3 %copy-start = (f32[256,1152]{1,0:T(8,128)S(1)}, f32[256,1152]{1,0:T(8,128)}, u32[]{:S(2)}) copy-start(f32[256,1152]{1,0:T(8,128)} %images.7) | copy-start | bytes 3538948
  1.9 1.3 %copy-start.2 = (f32[256,1152]{1,0:T(8,128)S(1)}, f32[256,1152]{1,0:T(8,128)}, u32[]{:S(2)}) copy-start(f32[256,1152]{1,0:T(8,128)} %texts.7) | copy-start | bytes 3538948
  4.0 24.3 %collective-permute-start = (bf16[256,1152]{1,0:T(8,128)(2,1)S(1)}, bf16[256,1152]{1,0:T(8,128)(2,1)S(1)}, u32[]{:S(2)}, u32[]{:S(2)}) collective-permute-start(bf16[256,1152]{1,0:T(8,128)(2,1)S(1)} %get-tuple-element.18.u), channel_id=1, source_target_pairs={{0,158},{1,3},{2,0},{3,5},{4,2},{5,7},{6,4},{7,9},{8,6},{9,11},{10... | collective-permute-start | bytes 1769480 | tf_op jit(solution)/shard_map/ppermute | solution.py:62
  8.0 30.4 %collective-permute-start.6 = (bf16[256,1152]{1,0:T(8,128)(2,1)S(1)}, bf16[256,1152]{1,0:T(8,128)(2,1)S(1)}, u32[]{:S(2)}, u32[]{:S(2)}) collective-permute-start(bf16[256,1152]{1,0:T(8,128)(2,1)S(1)} %get-tuple-element.18.u), channel_id=1, source_target_pairs={{2,767},{13,16},{18,15},{29,32},{34,31},{45,48},{50,47},{61,64},{6... | collective-permute-start | bytes 1769480 | tf_op jit(solution)/shard_map/ppermute | solution.py:62
  9.6 44.5 %collective-permute-start.8 = (bf16[256,1152]{1,0:T(8,128)(2,1)S(1)}, bf16[256,1152]{1,0:T(8,128)(2,1)S(1)}, u32[]{:S(2)}, u32[]{:S(2)}) collective-permute-start(bf16[256,1152]{1,0:T(8,128)(2,1)S(1)} %get-tuple-element.19.v), channel_id=1, source_target_pairs={{0,2},{1,767},{2,4},{3,1},{4,6},{5,3},{6,8},{7,5},{8,10},{9,7},{10... | collective-permute-start | bytes 1769480 | tf_op jit(solution)/shard_map/ppermute | solution.py:62
  28.3 31.6 %collective-permute-start.2 = (bf16[256,1152]{1,0:T(8,128)(2,1)S(1)}, bf16[256,1152]{1,0:T(8,128)(2,1)S(1)}, u32[]{:S(2)}, u32[]{:S(2)}) collective-permute-start(bf16[256,1152]{1,0:T(8,128)(2,1)S(1)} %collective-permute-done.refs_1_.near), channel_id=1, source_target_pairs={{158,766},{1,17},{30,14},{17,33},{46,30},{81,49},{14,46},{49,65},{... | collective-permute-start | bytes 1769480 | tf_op jit(solution)/shard_map/ppermute | solution.py:62
  33.7 26.2 %collective-permute-start.4 = (bf16[256,1152]{1,0:T(8,128)(2,1)S(1)}, bf16[256,1152]{1,0:T(8,128)(2,1)S(1)}, u32[]{:S(2)}, u32[]{:S(2)}) collective-permute-start(bf16[256,1152]{1,0:T(8,128)(2,1)S(1)} %shard_map.70), channel_id=1, source_target_pairs={{0,1},{1,0},{2,3},{3,2},{4,5},{5,4},{6,7},{7,6},{8,9},{9,8},{10,11... | collective-permute-start | bytes 1769480 | tf_op jit(solution)/shard_map/ppermute | solution.py:62
  37.1 22.8 %collective-permute-start.1 = (bf16[256,1152]{1,0:T(8,128)(2,1)S(1)}, bf16[256,1152]{1,0:T(8,128)(2,1)S(1)}, u32[]{:S(2)}, u32[]{:S(2)}) collective-permute-start(bf16[256,1152]{1,0:T(8,128)(2,1)S(1)} %collective-permute-done.refs_1_.near), channel_id=1, source_target_pairs={{0,1},{2,3},{3,2},{4,5},{5,4},{6,7},{7,6},{8,9},{9,8},{10,11},{11,... | collective-permute-start | bytes 1769480 | tf_op jit(solution)/shard_map/ppermute | solution.py:62
  38.4 24.4 %collective-permute-start.3 = (bf16[256,1152]{1,0:T(8,128)(2,1)S(1)}, bf16[256,1152]{1,0:T(8,128)(2,1)S(1)}, u32[]{:S(2)}, u32[]{:S(2)}) collective-permute-start(bf16[256,1152]{1,0:T(8,128)(2,1)S(1)} %collective-permute-done.refs_1_.near), channel_id=1, source_target_pairs={{2,1},{3,4},{4,3},{5,6},{6,5},{7,8},{8,7},{9,10},{10,9},{11,12},{1... | collective-permute-start | bytes 1769480 | tf_op jit(solution)/shard_map/ppermute | solution.py:62
  54.1 11.4 %collective-permute-start.9 = (bf16[256,1152]{1,0:T(8,128)(2,1)S(1)}, bf16[256,1152]{1,0:T(8,128)(2,1)S(1)}, u32[]{:S(2)}, u32[]{:S(2)}) collective-permute-start(bf16[256,1152]{1,0:T(8,128)(2,1)S(1)} %shard_map.73.across), channel_id=1, source_target_pairs={{0,1},{1,0},{2,3},{3,2},{4,5},{5,4},{6,7},{7,6},{8,9},{9,8},{10,11... | collective-permute-start | bytes 1769480 | tf_op jit(solution)/shard_map/ppermute | solution.py:62
  59.9 5.6 %copy-start.1 = (f32[256,1152]{1,0:T(8,128)S(1)}, f32[256,1152]{1,0:T(8,128)}, u32[]{:S(2)}) copy-start(f32[256,1152]{1,0:T(8,128)} %images.7) | copy-start | bytes 3538948
  59.9 5.6 %copy-start.3 = (f32[256,1152]{1,0:T(8,128)S(1)}, f32[256,1152]{1,0:T(8,128)}, u32[]{:S(2)}) copy-start(f32[256,1152]{1,0:T(8,128)} %texts.7) | copy-start | bytes 3538948
  62.8 7.3 %collective-permute-start.5 = (bf16[256,1152]{1,0:T(8,128)(2,1)S(1)}, bf16[256,1152]{1,0:T(8,128)(2,1)S(1)}, u32[]{:S(2)}, u32[]{:S(2)}) collective-permute-start(bf16[256,1152]{1,0:T(8,128)(2,1)S(1)} %shard_map.71.turned), channel_id=1, source_target_pairs={{1,0},{14,15},{17,16},{30,31},{33,32},{46,47},{49,48},{62,63},{65,... | collective-permute-start | bytes 1769480 | tf_op jit(solution)/shard_map/ppermute | solution.py:62
  64.1 8.1 %collective-permute-start.7 = (bf16[256,1152]{1,0:T(8,128)(2,1)S(1)}, bf16[256,1152]{1,0:T(8,128)(2,1)S(1)}, u32[]{:S(2)}, u32[]{:S(2)}) collective-permute-start(bf16[256,1152]{1,0:T(8,128)(2,1)S(1)} %shard_map.71.turned), channel_id=1, source_target_pairs={{1,2},{14,13},{17,18},{30,29},{33,34},{46,45},{49,50},{62,61},{65,... | collective-permute-start | bytes 1769480 | tf_op jit(solution)/shard_map/ppermute | solution.py:62

commit v5 on v4

--- a/solution.py
+++ b/solution.py
@@ -278,7 +278,7 @@
     passed_across = send(across, pairs["swap"])
     turned = after(turned, flops=35 * 10**8)
     turned = after(turned, far, passed_near, beside)
-    far_turned = send(turned, pairs["far_turned"])
+    far_turned = after(send(turned, pairs["far_turned"]), flops=2 * 10**9)
     passed_turned = send(turned, pairs["pass_turned"])
     grad_u, grad_v, loss_u, loss_v = pl.pallas_call(
         second_kernel,

time: 77.1 us -> 76.3 us (0.990)
  waiting for transfers between devices: 20.5 us -> 19.2 us
    ppermute x10, waiting for transfers between devices: 20.5 us -> 19.2 us  [send(): return lax.ppermute(value, AXES, pairs)]
where the time goes in v5:
time: 76.3 us; the launch traced here: 75.9 us
  starting transfers between devices  39 us (51%)
  waiting for transfers between devices  19.2 us (25%)
  Pallas kernels  12.9 us (17%)
  local copies, waits for them, and re-layouts  2.59 us (3%)
  between operations  2.11 us (3%)
    ppermute x10, starting transfers between devices, send(): return lax.ppermute(value, AXES, pairs)  39 us
    ppermute x10, waiting for transfers between devices, send(): return lax.ppermute(value, AXES, pairs)  19.2 us
    pallas_call x1, Pallas kernels, local(): pl.pallas_call(second_kernel, out_shape=(wide, wide, column, column), in_...  4.65 us
    pallas_call x1, Pallas kernels, local(): pl.pallas_call(last_kernel, out_shape=(jax.ShapeDtypeStruct((1, count), W...  4.52 us
    unnamed x9, local copies, waits for them, and re-layouts  2.59 us
    pallas_call x1, Pallas kernels, local(): pl.pallas_call(first_kernel, out_shape=(wide, wide, column, column), in_s...  2.06 us
    pallas_call x2, Pallas kernels, unit(): pl.pallas_call(functools.partial(unit_kernel, swap), out_shape=(half, col...  1.63 us
  transfers between devices with their start and end apart: 10, of which 4 were waited for; matrix products, arithmetic and copies ran while one was open for 0% of the time, Pallas kernels for 10%

profile of v5, /device:TPU:1, one launch (start us, length us, event | category | flops | bytes accessed | tf_op | source)
XLA Modules:
  0.0 75.9 jit_solution(16690949037667028424)
XLA Ops:
  0.6 0.0 copy-start
  0.6 1.3 %copy-done = f32[256,1152]{1,0:T(8,128)S(1)} copy-done((f32[256,1152]{1,0:T(8,128)S(1)}, f32[256,1152]{1,0:T(8,128)}, u32[]{:S(2)}) %copy-start) | copy-done | bytes 1179672
  1.9 0.0 copy-start.2
  1.9 1.3 %copy-done.2 = f32[256,1152]{1,0:T(8,128)S(1)} copy-done((f32[256,1152]{1,0:T(8,128)S(1)}, f32[256,1152]{1,0:T(8,128)}, u32[]{:S(2)}) %copy-start.2) | copy-done | bytes 1179672
  3.2 0.8 %shard_map.67 = (bf16[256,1152]{1,0:T(8,128)(2,1)S(1)}, f32[256,1]{1,0:T(8,128)S(1)}) custom-call(f32[256,1152]{1,0:T(8,128)S(1)} %copy-done, f32[256,1152]{1,0:T(8,128)S(1)} %copy-done.2), custom_call_target="tpu_custom_call" | custom-call | tf_op jit(solution)/shard_map/pallas_call | solution.py:250
  4.0 4.0 %collective-permute-start = (bf16[256,1152]{1,0:T(8,128)(2,1)S(1)}, bf16[256,1152]{1,0:T(8,128)(2,1)S(1)}, u32[]{:S(2)}, u32[]{:S(2)}) collective-permute-start(bf16[256,1152]{1,0:T(8,128)(2,1)S(1)} %get-tuple-element.18.u), channel_id=1, source_target_pairs={{0,158},{1,3},{2,0},{3,5},{4,2},{5,7},{6,4},{7,9},{8,6},{9,11},{10... | collective-permute-start | bytes 1769480 | tf_op jit(solution)/shard_map/ppermute | solution.py:62
  8.0 0.7 collective-permute-start.6
  8.7 0.8 %shard_map.69 = (bf16[256,1152]{1,0:T(8,128)(2,1)S(1)}, f32[256,1]{1,0:T(8,128)S(1)}) custom-call(f32[256,1152]{1,0:T(8,128)S(1)} %copy-done, f32[256,1152]{1,0:T(8,128)S(1)} %copy-done.2), custom_call_target="tpu_custom_call" | custom-call | tf_op jit(solution)/shard_map/pallas_call | solution.py:250
  9.6 18.7 %collective-permute-start.8 = (bf16[256,1152]{1,0:T(8,128)(2,1)S(1)}, bf16[256,1152]{1,0:T(8,128)(2,1)S(1)}, u32[]{:S(2)}, u32[]{:S(2)}) collective-permute-start(bf16[256,1152]{1,0:T(8,128)(2,1)S(1)} %get-tuple-element.19.v), channel_id=1, source_target_pairs={{0,2},{1,767},{2,4},{3,1},{4,6},{5,3},{6,8},{7,5},{8,10},{9,7},{10... | collective-permute-start | bytes 1769480 | tf_op jit(solution)/shard_map/ppermute | solution.py:62
  28.3 0.0 collective-permute-done.refs_1_.near
  28.3 1.9 %collective-permute-start.2 = (bf16[256,1152]{1,0:T(8,128)(2,1)S(1)}, bf16[256,1152]{1,0:T(8,128)(2,1)S(1)}, u32[]{:S(2)}, u32[]{:S(2)}) collective-permute-start(bf16[256,1152]{1,0:T(8,128)(2,1)S(1)} %collective-permute-done.refs_1_.near), channel_id=1, source_target_pairs={{158,766},{1,17},{30,14},{17,33},{46,30},{81,49},{14,46},{49,65},{... | collective-permute-start | bytes 1769480 | tf_op jit(solution)/shard_map/ppermute | solution.py:62
  31.6 0.1 pad_maximum_fusion.consts
  31.7 2.1 %shard_map.73 = (f32[256,1152]{1,0:T(8,128)S(1)}, f32[256,1152]{1,0:T(8,128)S(1)}, f32[256,1]{1,0:T(8,128)S(1)}, f32[256,1]{1,0:T(8,128)S(1)}) custom-call(f32[2]{0:T(128)S(1)} %pad_maximum_fusion.consts, bf16[256,1152]{1,0:T(8,128)(2,1)S(1)} %get-tuple-element.18.u, bf16[256,1152]{1,0:T(8,128)(2,1)S(1)} %get-tuple-element.19.v), custom_call_target="tpu_custom_call" | custom-call | flops 301989888 | bytes 4194304 | tf_op jit(solution)/shard_map/pallas_call | solution.py:268
  33.7 3.4 %collective-permute-start.4 = (bf16[256,1152]{1,0:T(8,128)(2,1)S(1)}, bf16[256,1152]{1,0:T(8,128)(2,1)S(1)}, u32[]{:S(2)}, u32[]{:S(2)}) collective-permute-start(bf16[256,1152]{1,0:T(8,128)(2,1)S(1)} %shard_map.70), channel_id=1, source_target_pairs={{0,1},{1,0},{2,3},{3,2},{4,5},{5,4},{6,7},{7,6},{8,9},{9,8},{10,11... | collective-permute-start | bytes 1769480 | tf_op jit(solution)/shard_map/ppermute | solution.py:62
  37.1 1.3 %collective-permute-start.1 = (bf16[256,1152]{1,0:T(8,128)(2,1)S(1)}, bf16[256,1152]{1,0:T(8,128)(2,1)S(1)}, u32[]{:S(2)}, u32[]{:S(2)}) collective-permute-start(bf16[256,1152]{1,0:T(8,128)(2,1)S(1)} %collective-permute-done.refs_1_.near), channel_id=1, source_target_pairs={{0,1},{2,3},{3,2},{4,5},{5,4},{6,7},{7,6},{8,9},{9,8},{10,11},{11,... | collective-permute-start | bytes 1769480 | tf_op jit(solution)/shard_map/ppermute | solution.py:62
  38.4 0.0 collective-permute-done.6.refs_1_.leap
  38.4 1.3 %collective-permute-start.3 = (bf16[256,1152]{1,0:T(8,128)(2,1)S(1)}, bf16[256,1152]{1,0:T(8,128)(2,1)S(1)}, u32[]{:S(2)}, u32[]{:S(2)}) collective-permute-start(bf16[256,1152]{1,0:T(8,128)(2,1)S(1)} %collective-permute-done.refs_1_.near), channel_id=1, source_target_pairs={{2,1},{3,4},{4,3},{5,6},{6,5},{7,8},{8,7},{9,10},{10,9},{11,12},{1... | collective-permute-start | bytes 1769480 | tf_op jit(solution)/shard_map/ppermute | solution.py:62
  39.7 14.3 %collective-permute-done.8.refs_0_ = bf16[256,1152]{1,0:T(8,128)(2,1)S(1)} collective-permute-done((bf16[256,1152]{1,0:T(8,128)(2,1)S(1)}, bf16[256,1152]{1,0:T(8,128)(2,1)S(1)}, u32[]{:S(2)}, u32[]{:S(2)}) %collective-permute-start.8) | collective-permute-done | bytes 589856 | tf_op jit(solution)/shard_map/ppermute | solution.py:62
  54.1 4.6 %collective-permute-start.9 = (bf16[256,1152]{1,0:T(8,128)(2,1)S(1)}, bf16[256,1152]{1,0:T(8,128)(2,1)S(1)}, u32[]{:S(2)}, u32[]{:S(2)}) collective-permute-start(bf16[256,1152]{1,0:T(8,128)(2,1)S(1)} %shard_map.74.across), channel_id=1, source_target_pairs={{0,1},{1,0},{2,3},{3,2},{4,5},{5,4},{6,7},{7,6},{8,9},{9,8},{10,11... | collective-permute-start | bytes 1769480 | tf_op jit(solution)/shard_map/ppermute | solution.py:62
  58.7 1.2 %collective-permute-done.2.refs_0_ = bf16[256,1152]{1,0:T(8,128)(2,1)S(1)} collective-permute-done((bf16[256,1152]{1,0:T(8,128)(2,1)S(1)}, bf16[256,1152]{1,0:T(8,128)(2,1)S(1)}, u32[]{:S(2)}, u32[]{:S(2)}) %collective-permute-start.2) | collective-permute-done | bytes 589856 | tf_op jit(solution)/shard_map/ppermute | solution.py:62
  59.9 0.0 copy-start.1
  59.9 0.0 copy-start.3
  59.9 0.0 collective-permute-done.4.refs_3_.beside
  59.9 0.0 collective-permute-done.1.refs_2_.passed
  59.9 2.9 %collective-permute-done.3.refs_1_.far = bf16[256,1152]{1,0:T(8,128)(2,1)S(1)} collective-permute-done((bf16[256,1152]{1,0:T(8,128)(2,1)S(1)}, bf16[256,1152]{1,0:T(8,128)(2,1)S(1)}, u32[]{:S(2)}, u32[]{:S(2)}) %collective-permute-start.3) | collective-permute-done | bytes 589856 | tf_op jit(solution)/shard_map/ppermute | solution.py:62
  62.8 1.8 %collective-permute-start.7 = (bf16[256,1152]{1,0:T(8,128)(2,1)S(1)}, bf16[256,1152]{1,0:T(8,128)(2,1)S(1)}, u32[]{:S(2)}, u32[]{:S(2)}) collective-permute-start(bf16[256,1152]{1,0:T(8,128)(2,1)S(1)} %shard_map.71.turned), channel_id=1, source_target_pairs={{1,2},{14,13},{17,18},{30,29},{33,34},{46,45},{49,50},{62,61},{65,... | collective-permute-start | bytes 1769480 | tf_op jit(solution)/shard_map/ppermute | solution.py:62
  64.6 1.3 %collective-permute-start.5 = (bf16[256,1152]{1,0:T(8,128)(2,1)S(1)}, bf16[256,1152]{1,0:T(8,128)(2,1)S(1)}, u32[]{:S(2)}, u32[]{:S(2)}) collective-permute-start(bf16[256,1152]{1,0:T(8,128)(2,1)S(1)} %shard_map.71.turned), channel_id=1, source_target_pairs={{1,0},{14,15},{17,16},{30,31},{33,32},{46,47},{49,48},{62,63},{65,... | collective-permute-start | bytes 1769480 | tf_op jit(solution)/shard_map/ppermute | solution.py:62
  65.9 0.0 collective-permute-done.9.passed
  65.9 0.0 copy-done.1
  65.9 0.0 copy-done.3
  65.9 4.7 %shard_map.75 = (f32[256,1152]{1,0:T(8,128)S(1)}, f32[256,1152]{1,0:T(8,128)S(1)}, f32[256,1]{1,0:T(8,128)S(1)}, f32[256,1]{1,0:T(8,128)S(1)}) custom-call(f32[2]{0:T(128)S(1)} %pad_maximum_fusion.consts, bf16[256,1152]{1,0:T(8,128)(2,1)S(1)} %get-tuple-element.18.u, bf16[256,1152]{1,0:T(8,128)(2,1)S(1)} %get-tuple-element.19.v, ...), custom_call_target="tpu_custom_call" | custom-call | flops 9059696640 | bytes 4194304 | tf_op jit(solution)/shard_map/pallas_call | solution.py:283
  70.6 0.7 collective-permute-done.7.refs_0_
  71.3 0.0 collective-permute-done.5.passed_turned
  71.3 4.5 %shard_map.76 = (f32[1,256]{1,0:T(1,128)}, f32[256,1152]{1,0:T(8,128)}, f32[256,1152]{1,0:T(8,128)}) custom-call(f32[2]{0:T(128)S(1)} %pad_maximum_fusion.consts, bf16[256,1152]{1,0:T(8,128)(2,1)S(1)} %get-tuple-element.18.u, bf16[256,1152]{1,0:T(8,128)(2,1)S(1)} %collective-permute-done.1.refs_2_.passed, ...), custom_call_target="tpu_custom_call" | custom-call | flops 6039797760 | bytes 4194304 | tf_op jit(solution)/shard_map/pallas_call | solution.py:292
  (6 shorter events, 0.1 us)
Async XLA Ops:
  0.6 1.3 %copy-start = (f32[256,1152]{1,0:T(8,128)S(1)}, f32[256,1152]{1,0:T(8,128)}, u32[]{:S(2)}) copy-start(f32[256,1152]{1,0:T(8,128)} %images.7) | copy-start | bytes 3538948
  1.9 1.3 %copy-start.2 = (f32[256,1152]{1,0:T(8,128)S(1)}, f32[256,1152]{1,0:T(8,128)}, u32[]{:S(2)}) copy-start(f32[256,1152]{1,0:T(8,128)} %texts.7) | copy-start | bytes 3538948
  4.0 24.3 %collective-permute-start = (bf16[256,1152]{1,0:T(8,128)(2,1)S(1)}, bf16[256,1152]{1,0:T(8,128)(2,1)S(1)}, u32[]{:S(2)}, u32[]{:S(2)}) collective-permute-start(bf16[256,1152]{1,0:T(8,128)(2,1)S(1)} %get-tuple-element.18.u), channel_id=1, source_target_pairs={{0,158},{1,3},{2,0},{3,5},{4,2},{5,7},{6,4},{7,9},{8,6},{9,11},{10... | collective-permute-start | bytes 1769480 | tf_op jit(solution)/shard_map/ppermute | solution.py:62
  8.0 30.4 %collective-permute-start.6 = (bf16[256,1152]{1,0:T(8,128)(2,1)S(1)}, bf16[256,1152]{1,0:T(8,128)(2,1)S(1)}, u32[]{:S(2)}, u32[]{:S(2)}) collective-permute-start(bf16[256,1152]{1,0:T(8,128)(2,1)S(1)} %get-tuple-element.18.u), channel_id=1, source_target_pairs={{2,767},{13,16},{18,15},{29,32},{34,31},{45,48},{50,47},{61,64},{6... | collective-permute-start | bytes 1769480 | tf_op jit(solution)/shard_map/ppermute | solution.py:62
  9.6 44.5 %collective-permute-start.8 = (bf16[256,1152]{1,0:T(8,128)(2,1)S(1)}, bf16[256,1152]{1,0:T(8,128)(2,1)S(1)}, u32[]{:S(2)}, u32[]{:S(2)}) collective-permute-start(bf16[256,1152]{1,0:T(8,128)(2,1)S(1)} %get-tuple-element.19.v), channel_id=1, source_target_pairs={{0,2},{1,767},{2,4},{3,1},{4,6},{5,3},{6,8},{7,5},{8,10},{9,7},{10... | collective-permute-start | bytes 1769480 | tf_op jit(solution)/shard_map/ppermute | solution.py:62
  28.3 31.6 %collective-permute-start.2 = (bf16[256,1152]{1,0:T(8,128)(2,1)S(1)}, bf16[256,1152]{1,0:T(8,128)(2,1)S(1)}, u32[]{:S(2)}, u32[]{:S(2)}) collective-permute-start(bf16[256,1152]{1,0:T(8,128)(2,1)S(1)} %collective-permute-done.refs_1_.near), channel_id=1, source_target_pairs={{158,766},{1,17},{30,14},{17,33},{46,30},{81,49},{14,46},{49,65},{... | collective-permute-start | bytes 1769480 | tf_op jit(solution)/shard_map/ppermute | solution.py:62
  33.7 26.2 %collective-permute-start.4 = (bf16[256,1152]{1,0:T(8,128)(2,1)S(1)}, bf16[256,1152]{1,0:T(8,128)(2,1)S(1)}, u32[]{:S(2)}, u32[]{:S(2)}) collective-permute-start(bf16[256,1152]{1,0:T(8,128)(2,1)S(1)} %shard_map.70), channel_id=1, source_target_pairs={{0,1},{1,0},{2,3},{3,2},{4,5},{5,4},{6,7},{7,6},{8,9},{9,8},{10,11... | collective-permute-start | bytes 1769480 | tf_op jit(solution)/shard_map/ppermute | solution.py:62
  37.1 22.8 %collective-permute-start.1 = (bf16[256,1152]{1,0:T(8,128)(2,1)S(1)}, bf16[256,1152]{1,0:T(8,128)(2,1)S(1)}, u32[]{:S(2)}, u32[]{:S(2)}) collective-permute-start(bf16[256,1152]{1,0:T(8,128)(2,1)S(1)} %collective-permute-done.refs_1_.near), channel_id=1, source_target_pairs={{0,1},{2,3},{3,2},{4,5},{5,4},{6,7},{7,6},{8,9},{9,8},{10,11},{11,... | collective-permute-start | bytes 1769480 | tf_op jit(solution)/shard_map/ppermute | solution.py:62
  38.4 24.4 %collective-permute-start.3 = (bf16[256,1152]{1,0:T(8,128)(2,1)S(1)}, bf16[256,1152]{1,0:T(8,128)(2,1)S(1)}, u32[]{:S(2)}, u32[]{:S(2)}) collective-permute-start(bf16[256,1152]{1,0:T(8,128)(2,1)S(1)} %collective-permute-done.refs_1_.near), channel_id=1, source_target_pairs={{2,1},{3,4},{4,3},{5,6},{6,5},{7,8},{8,7},{9,10},{10,9},{11,12},{1... | collective-permute-start | bytes 1769480 | tf_op jit(solution)/shard_map/ppermute | solution.py:62
  54.1 11.8 %collective-permute-start.9 = (bf16[256,1152]{1,0:T(8,128)(2,1)S(1)}, bf16[256,1152]{1,0:T(8,128)(2,1)S(1)}, u32[]{:S(2)}, u32[]{:S(2)}) collective-permute-start(bf16[256,1152]{1,0:T(8,128)(2,1)S(1)} %shard_map.74.across), channel_id=1, source_target_pairs={{0,1},{1,0},{2,3},{3,2},{4,5},{5,4},{6,7},{7,6},{8,9},{9,8},{10,11... | collective-permute-start | bytes 1769480 | tf_op jit(solution)/shard_map/ppermute | solution.py:62
  59.9 6.0 %copy-start.1 = (f32[256,1152]{1,0:T(8,128)S(1)}, f32[256,1152]{1,0:T(8,128)}, u32[]{:S(2)}) copy-start(f32[256,1152]{1,0:T(8,128)} %images.7) | copy-start | bytes 3538948
  59.9 6.0 %copy-start.3 = (f32[256,1152]{1,0:T(8,128)S(1)}, f32[256,1152]{1,0:T(8,128)}, u32[]{:S(2)}) copy-start(f32[256,1152]{1,0:T(8,128)} %texts.7) | copy-start | bytes 3538948
  62.8 8.5 %collective-permute-start.7 = (bf16[256,1152]{1,0:T(8,128)(2,1)S(1)}, bf16[256,1152]{1,0:T(8,128)(2,1)S(1)}, u32[]{:S(2)}, u32[]{:S(2)}) collective-permute-start(bf16[256,1152]{1,0:T(8,128)(2,1)S(1)} %shard_map.71.turned), channel_id=1, source_target_pairs={{1,2},{14,13},{17,18},{30,29},{33,34},{46,45},{49,50},{62,61},{65,... | collective-permute-start | bytes 1769480 | tf_op jit(solution)/shard_map/ppermute | solution.py:62
  64.6 6.8 %collective-permute-start.5 = (bf16[256,1152]{1,0:T(8,128)(2,1)S(1)}, bf16[256,1152]{1,0:T(8,128)(2,1)S(1)}, u32[]{:S(2)}, u32[]{:S(2)}) collective-permute-start(bf16[256,1152]{1,0:T(8,128)(2,1)S(1)} %shard_map.71.turned), channel_id=1, source_target_pairs={{1,0},{14,15},{17,16},{30,31},{33,32},{46,47},{49,48},{62,63},{65,... | collective-permute-start | bytes 1769480 | tf_op jit(solution)/shard_map/ppermute | solution.py:62
